TPU v7x, 32 devices: a whole 2x2x4 slice. The times are simulated.
32 devices in a mesh: group: 4 (over x, core), member: 8 (over z, y).
Axes of the slice: x: 2, y: 2, z: 4, core: 2. Of those that a mesh axis runs over, the one named last changes fastest.
Arguments:
- q_rows: bfloat16 [8192, 8192], P(('group', 'member')), may hold values from -36 to 36
- own_kv: bfloat16 [8192, 1024], P(('group', 'member')), may hold values from -6 to 6
- cache: bfloat16 [128, 64, 1024], P(('group', 'member')), may hold values from -6 to 6
- recomp_hidden: bfloat16 [64, 8, 16, 4096], P(('group', 'member')), may hold values from -6 to 6
- w_kv: bfloat16 [4096, 1024], P('member', 'group'), may hold values from -0.09375 to 0.09375
- retrieval: int32 [64, 8], P(('group', 'member')), may hold values from 0 to 31, as said below
- positions: int32 [64, 8, 16], P(('group', 'member')), may hold values from 0 to 63, as said below
Outputs:
- attn_out: bfloat16 [8192, 8192], P(('group', 'member'))
Inputs may be any that keep to these rules, and one draw needn't show every extreme that they name: `retrieval`: the 8 passages of one query are different. Passage i of a group's corpus is held by the device of member index i // 4 in that group. The queries of one device name at most 2 passages held by any one device, and this bound is reached. The 16 positions of one retrieved passage are different.
All inputs are finite; a program needn't handle non-finite values.
Results may differ from a plain program's by a relative error of at most 0.0054.
Values may be sent and summed in bfloat16 or wider, within the bound.
No kernel may reach another device: no remote copies, remote signals or barrier semaphores. Data moves between devices by JAX's collectives and lax.ppermute only.
A program may use at most 128 MiB of HBM per device.

v0:
```python
import functools

import jax
import jax.numpy as jnp
from jax import lax
from jax.experimental import pallas as pl
from jax.experimental.pallas import tpu as pltpu
from jax.sharding import PartitionSpec as P

D = 4096
HQ = 64
KVH = 4
HD = 128
TOPP = 8
QLEN = 128
PLEN = 64
RECOMP = 16
KEPT = PLEN - RECOMP
GROUPED = HQ // KVH
PAIRS = 2
PAIR_HEADS = KVH // PAIRS
PAIR_WIDTH = PAIR_HEADS * HD
HALF = KVH * HD

EPSILON = 1e-06
SCORE_FACTOR = 1.4426950408889634 / HD**0.5
SAFE_EXPONENT = 80.0
VMEM_BYTES = 56 * 1024 * 1024
LITTLE = pl.CostEstimate(flops=1, bytes_accessed=1, transcendentals=0)
MEDIUM = pl.CostEstimate(flops=1, bytes_accessed=18_000_000, transcendentals=0)
LARGE = pl.CostEstimate(flops=1, bytes_accessed=36_000_000, transcendentals=0)


def norm_kernel(hidden_ref, *rest):
    normed_ref = rest[-1]
    hidden = hidden_ref[...].astype(jnp.float32)
    mean = jnp.mean(hidden * hidden, axis=1, keepdims=True)
    normed_ref[...] = (hidden * lax.rsqrt(mean + EPSILON)).astype(jnp.bfloat16)


def normalise(hidden, ahead):
    rows = hidden.shape[0]
    tile = min(rows, 64)
    return pl.pallas_call(
        norm_kernel,
        grid=(rows // tile,),
        in_specs=[pl.BlockSpec((tile, D), lambda i: (i, 0))] + [pl.BlockSpec(memory_space=pl.ANY)] * len(ahead),
        out_specs=pl.BlockSpec((tile, D), lambda i: (i, 0)),
        out_shape=jax.ShapeDtypeStruct(hidden.shape, jnp.bfloat16),
        compiler_params=pltpu.CompilerParams(vmem_limit_bytes=VMEM_BYTES),
        cost_estimate=LITTLE,
        name="normalise",
    )(hidden, *ahead)


def find_kernel(holders, requests, pass_local, capacity, me_ref, table_ref, rank_ref, passage_ref, slot_ref, kept_ref):
    me = me_ref[0]
    stride = table_ref.shape[0] // holders
    for k in range(holders):
        base = k * (capacity + 1)
        for rank in range(capacity + 1):
            slot_ref[base + rank] = 0
        count = jnp.int32(0)
        for request in range(requests):
            slot_ref[base + count] = request
            mine = (table_ref[k * stride + request] // pass_local == me).astype(jnp.int32)
            count = jnp.minimum(count + mine, capacity)
    spot = lax.broadcasted_iota(jnp.int32, (1, PLEN), 1)
    for k in range(holders):
        for rank in range(capacity):
            at = k * capacity + rank
            request = slot_ref[k * (capacity + 1) + rank]
            passage_ref[at] = lax.rem(table_ref[k * stride + request], pass_local)
            start = k * stride + requests + request * RECOMP
            covered = spot < 0
            for r in range(RECOMP):
                covered = covered | (spot == table_ref[start + r])
            kept_ref[at : at + 1, :] = jnp.where(covered, 0.0, 1.0)
    kept = kept_ref[...]
    upto = lax.broadcasted_iota(jnp.int32, (PLEN, PLEN), 0) <= lax.broadcasted_iota(jnp.int32, (PLEN, PLEN), 1)
    rank_of = jnp.dot(
        kept.astype(jnp.bfloat16), upto.astype(jnp.bfloat16), preferred_element_type=jnp.float32
    )
    rank_ref[...] = jnp.where(kept > 0, rank_of, 0.0)


def find_rows(table, me, holders, requests, pass_local, capacity):
    slots = holders * capacity
    smem = pl.BlockSpec(memory_space=pltpu.SMEM)
    return pl.pallas_call(
        functools.partial(find_kernel, holders, requests, pass_local, capacity),
        in_specs=[smem, smem],
        out_specs=[pl.BlockSpec(memory_space=pltpu.VMEM), smem],
        out_shape=[jax.ShapeDtypeStruct((slots, PLEN), jnp.float32), jax.ShapeDtypeStruct((slots,), jnp.int32)],
        scratch_shapes=[pltpu.SMEM((holders * (capacity + 1),), jnp.int32), pltpu.VMEM((slots, PLEN), jnp.float32)],
        compiler_params=pltpu.CompilerParams(vmem_limit_bytes=VMEM_BYTES),
        cost_estimate=LARGE,
        name="find_rows",
    )(me, table)


def pick_kernel(me_ref, passage_ref, rank_ref, cache_ref, *rest):
    out_ref = rest[-1]
    pair = me_ref[1]
    row = (lax.broadcasted_iota(jnp.int32, (KEPT, PLEN), 0) + 1).astype(jnp.float32)
    for at in range(out_ref.shape[0]):
        passage = passage_ref[at]
        select = (rank_ref[at : at + 1, :] == row).astype(jnp.bfloat16)
        for place, part in ((0, pair), (1, 1 - pair)):
            for half in range(2):
                start = pl.multiple_of(half * HALF + part * PAIR_WIDTH, PAIR_WIDTH)
                end = (place * 2 + half) * PAIR_WIDTH
                out_ref[at, :, end : end + PAIR_WIDTH] = jnp.dot(
                    select, cache_ref[passage, :, pl.ds(start, PAIR_WIDTH)], preferred_element_type=jnp.float32
                ).astype(jnp.bfloat16)


def pick_rows(me, passages, ranks, cache, ahead):
    smem = pl.BlockSpec(memory_space=pltpu.SMEM)
    vmem = pl.BlockSpec(memory_space=pltpu.VMEM)
    return pl.pallas_call(
        pick_kernel,
        in_specs=[smem, smem, vmem, vmem] + [pl.BlockSpec(memory_space=pl.ANY)] * len(ahead),
        out_specs=vmem,
        out_shape=jax.ShapeDtypeStruct((passages.shape[0], KEPT, 2 * HALF), jnp.bfloat16),
        compiler_params=pltpu.CompilerParams(vmem_limit_bytes=VMEM_BYTES),
        cost_estimate=LITTLE,
        name="pick_rows",
    )(me, passages, ranks, cache, *ahead)


def project_kernel(chunks, wanted, carried, last, member_ref, mine_ref, other_ref, *refs):
    weights, total_ref = refs[: len(wanted)], refs[len(wanted)]
    rows = mine_ref.shape[0]
    depth = D // chunks
    total = total_ref[...] if carried else None
    for k, weight_ref in zip(wanted, weights):
        columns = pl.ds(pl.multiple_of((member_ref[0] ^ k) * depth, depth), depth)
        both = jnp.concatenate([mine_ref[:, columns], other_ref[:, columns]], axis=0)
        term = jnp.dot(both, weight_ref[...], preferred_element_type=jnp.float32)
        total = term if total is None else total + term
    if last:
        refs[-2][...] = total[:rows].astype(jnp.bfloat16)
        refs[-1][...] = total[rows:].astype(jnp.bfloat16)
    else:
        refs[-1][...] = total


def project(member, mine, other, weights, wanted, ahead, carry=None, last=True):
    rows, width = mine.shape[0], weights[0].shape[1]
    vmem = pl.BlockSpec(memory_space=pltpu.VMEM)
    carried = [] if carry is None else [carry]
    if last:
        shape = [jax.ShapeDtypeStruct((rows, width), jnp.bfloat16)] * 2
    else:
        shape = [jax.ShapeDtypeStruct((2 * rows, width), jnp.float32)]
    return pl.pallas_call(
        functools.partial(project_kernel, len(weights), wanted, bool(carried), last),
        in_specs=[pl.BlockSpec(memory_space=pltpu.SMEM)]
        + [vmem] * (2 + len(wanted) + len(carried))
        + [pl.BlockSpec(memory_space=pl.ANY)] * len(ahead),
        out_specs=[vmem] * len(shape),
        out_shape=shape,
        compiler_params=pltpu.CompilerParams(vmem_limit_bytes=VMEM_BYTES),
        cost_estimate=MEDIUM,
        name="project",
    )(member.reshape(1), mine, other, *[weights[k] for k in wanted], *carried, *ahead)


def bound_kernel(q_ref, *rest):
    bound_ref = rest[-1]

    @pl.when(pl.program_id(0) == 0)
    def clear():
        bound_ref[...] = jnp.zeros_like(bound_ref)

    peak = jnp.zeros((q_ref.shape[0], 1), jnp.float32)
    for first in range(0, GROUPED, 4):
        most = None
        for head in range(first, first + 4):
            block = q_ref[:, head * HD : (head + 1) * HD].astype(jnp.float32)
            most = block * block if most is None else jnp.maximum(most, block * block)
        peak = jnp.maximum(peak, jnp.sum(most, axis=1, keepdims=True))
    bound_ref[...] = jnp.maximum(bound_ref[...], jnp.max(peak))


def query_bound(q_rows, ahead):
    rows, width = q_rows.shape
    return pl.pallas_call(
        bound_kernel,
        grid=(KVH,),
        in_specs=[pl.BlockSpec((rows, GROUPED * HD), lambda h: (0, h))]
        + [pl.BlockSpec(memory_space=pl.ANY)] * len(ahead),
        out_specs=pl.BlockSpec((8, HD), lambda h: (0, 0)),
        out_shape=jax.ShapeDtypeStruct((8, HD), jnp.float32),
        compiler_params=pltpu.CompilerParams(vmem_limit_bytes=VMEM_BYTES),
        cost_estimate=LITTLE,
        name="query_bound",
    )(q_rows, *ahead)


def attend_kernel(
    heads_once, info_ref, q_ref, own_k_ref, own_v_ref, kept_ref, near_ref, far_ref, bound_ref, *rest
):
    out_ref, key_ref, turned_ref, value_ref = rest[-4:]
    query = pl.program_id(0)
    key_start = pl.multiple_of(pl.program_id(1) * HD, HD)
    value_start = pl.multiple_of(PAIR_WIDTH + pl.program_id(1) * HD, HD)
    passage_keys = TOPP * PLEN
    flip = info_ref[1] > 0
    value_ref[:, HD:] = jnp.ones((passage_keys + QLEN, HD), jnp.bfloat16)
    for j in range(TOPP):
        slot = info_ref[2 + query * TOPP + j]
        key_ref[j * KEPT : (j + 1) * KEPT, :] = kept_ref[slot, :, pl.ds(key_start, HD)]
        value_ref[j * KEPT : (j + 1) * KEPT, :HD] = kept_ref[slot, :, pl.ds(value_start, HD)]
    key_ref[TOPP * KEPT : passage_keys, :] = jnp.where(flip, far_ref[...], near_ref[...])
    value_ref[TOPP * KEPT : passage_keys, :HD] = jnp.where(flip, near_ref[...], far_ref[...])
    key_ref[passage_keys:, :] = own_k_ref[...]
    value_ref[passage_keys:, :HD] = own_v_ref[...]
    scaled = key_ref[...].astype(jnp.float32) * SCORE_FACTOR
    high = scaled.astype(jnp.bfloat16)
    turned_ref[:HD, :] = high.T
    turned_ref[HD:, :] = (scaled - high.astype(jnp.float32)).astype(jnp.bfloat16).T
    key_bound = jnp.max(jnp.sum(scaled * scaled, axis=1, keepdims=True))
    small = jnp.max(bound_ref[...]) * key_bound <= SAFE_EXPONENT**2
    rows = heads_once * QLEN
    token = lax.broadcasted_iota(jnp.int32, (rows, QLEN), 0) % QLEN
    visible = lax.broadcasted_iota(jnp.int32, (rows, QLEN), 1) <= token

    def score(first):
        block = jnp.concatenate(
            [q_ref[:, (first + i) * HD : (first + i + 1) * HD] for i in range(heads_once)], axis=0
        )
        return jnp.dot(
            jnp.concatenate([block, block], axis=1), turned_ref[...], preferred_element_type=jnp.float32
        )

    def store(first, expd):
        summed = jnp.dot(expd, value_ref[...], preferred_element_type=jnp.float32)
        result = (summed[:, :HD] / summed[:, HD:]).astype(jnp.bfloat16)
        for i in range(heads_once):
            out_ref[:, (first + i) * HD : (first + i + 1) * HD] = result[i * QLEN : (i + 1) * QLEN]

    @pl.when(small)
    def unshifted():
        shown = jnp.where(visible, 1.0, 0.0).astype(jnp.bfloat16)
        for first in range(0, GROUPED, heads_once):
            expd = jnp.exp2(score(first)).astype(jnp.bfloat16)
            store(first, jnp.concatenate([expd[:, :passage_keys], expd[:, passage_keys:] * shown], axis=1))

    @pl.when(jnp.logical_not(small))
    def shifted():
        for first in range(0, GROUPED, heads_once):
            scores = score(first)
            scores = jnp.concatenate(
                [scores[:, :passage_keys], jnp.where(visible, scores[:, passage_keys:], -jnp.inf)], axis=1
            )
            peak = jnp.max(scores, axis=1, keepdims=True)
            store(first, jnp.exp2(scores - peak).astype(jnp.bfloat16))


def attend(part, info, q_rows, own_kv, kept, near, far, bound, earlier=None):
    rows, width = q_rows.shape
    queries = rows // QLEN
    slots = kept.shape[0]
    span = TOPP * PLEN + QLEN
    wide = GROUPED * HD
    in_specs = [
        pl.BlockSpec((QLEN, wide), lambda n, h, info: (n, info[0] * PAIR_HEADS + h)),
        pl.BlockSpec((QLEN, HD), lambda n, h, info: (n, info[0] * PAIR_HEADS + h)),
        pl.BlockSpec((QLEN, HD), lambda n, h, info: (n, KVH + info[0] * PAIR_HEADS + h)),
        pl.BlockSpec((slots, KEPT, HALF), lambda n, h, info: (0, 0, part)),
        pl.BlockSpec((TOPP * RECOMP, HD), lambda n, h, info: (n, h)),
        pl.BlockSpec((TOPP * RECOMP, HD), lambda n, h, info: (n, h)),
        pl.BlockSpec((8, HD), lambda n, h, info: (0, 0)),
    ]
    operands = [q_rows, own_kv, own_kv, kept, near, far, bound]
    aliases = {}
    if earlier is not None:
        in_specs.append(pl.BlockSpec(memory_space=pl.ANY))
        operands.append(earlier)
        aliases = {len(operands): 0}
    return pl.pallas_call(
        functools.partial(attend_kernel, 8),
        grid_spec=pltpu.PrefetchScalarGridSpec(
            num_scalar_prefetch=1,
            grid=(queries, PAIR_HEADS),
            in_specs=in_specs,
            out_specs=pl.BlockSpec((QLEN, wide), lambda n, h, info: (n, info[0] * PAIR_HEADS + h)),
            scratch_shapes=[
                pltpu.VMEM((span, HD), jnp.bfloat16),
                pltpu.VMEM((2 * HD, span), jnp.bfloat16),
                pltpu.VMEM((span, 2 * HD), jnp.bfloat16),
            ],
        ),
        out_shape=jax.ShapeDtypeStruct((rows, width), jnp.bfloat16),
        input_output_aliases=aliases,
        compiler_params=pltpu.CompilerParams(vmem_limit_bytes=VMEM_BYTES),
        cost_estimate=LITTLE,
        name="attend",
    )(info, *operands)


def swap(array, axis, bits):
    size = lax.axis_size(axis)
    return lax.ppermute(array, axis, [(i, i ^ bits) for i in range(size)])


def gather_columns(w_kv):
    column = [w_kv, swap(w_kv, "member", 2), swap(w_kv, "member", 4)]
    column.append(swap(column[2], "member", 2))
    across = [swap(part, "group", 2) for part in column]
    blocks, beyond = [], []
    for k in range(4):
        aside = swap(column[k], "member", 1)
        blocks += [column[k], aside]
        beyond += [across[k], swap(aside, "group", 2) if k < 3 else swap(across[k], "member", 1)]
    return blocks, beyond


def recompute_general(normed, w_kv, pair):
    whole = lax.all_gather(lax.all_gather(w_kv, "member", axis=0, tiled=True), "group", axis=1, tiled=True)
    result = jnp.dot(normed, whole, preferred_element_type=jnp.float32).astype(jnp.bfloat16)
    result = result.reshape(-1, 2, PAIRS, PAIR_WIDTH)
    first = jnp.where(pair == 0, result[:, :, 0], result[:, :, 1])
    second = jnp.where(pair == 0, result[:, :, 1], result[:, :, 0])
    return [first[:, 0], first[:, 1]], [second[:, 0], second[:, 1]]


def local(q_rows, own_kv, cache, recomp_hidden, w_kv, retrieval, positions):
    queries = retrieval.shape[0]
    requests = queries * TOPP
    holders = lax.axis_size("member")
    groups = lax.axis_size("group")
    pass_local = cache.shape[0]
    capacity = -(-requests // holders)
    member = lax.axis_index("member")
    group = lax.axis_index("group")
    pair = group % PAIRS
    tuned = groups == 4 and holders == 8
    wanted = retrieval.reshape(requests)
    request = jnp.concatenate([wanted, positions.reshape(requests * RECOMP)])
    request = jnp.pad(request, (0, -request.shape[0] % 128)).reshape(1, -1, 128)
    request = jnp.broadcast_to(request, (holders,) + request.shape[1:])
    table = lax.all_to_all(request, "member", split_axis=0, concat_axis=0, tiled=True).reshape(-1)
    hidden = recomp_hidden.reshape(requests * RECOMP, D)
    normed = normalise(hidden, [])
    ahead = [normed]
    if tuned:
        blocks, beyond = gather_columns(w_kv)
        ahead += [blocks[1], beyond[0], blocks[3], blocks[6], beyond[2]]
    me = jnp.stack([member, pair]).astype(jnp.int32)
    ranks, passages = find_rows(table, me, holders, requests, pass_local, capacity)
    sent = pick_rows(me, passages, ranks, cache, ahead)
    arrived = lax.all_to_all(
        sent.reshape(holders, capacity * KEPT, 2 * HALF), "member", split_axis=0, concat_axis=0, tiled=True
    ).reshape(sent.shape)
    bound = query_bound(q_rows, [sent])
    if tuned:
        flip = group // 2
        other = swap(normed, "group", 1)
        (begun,) = project(member, normed, other, beyond, (0, 2, 1, 4), [sent], last=False)
        near, near_other = project(member, normed, other, blocks, tuple(range(8)), [begun])
        far, far_other = project(member, normed, other, beyond, (6, 3, 5, 7), [near], carry=begun)
        first = [near, far]
        second = [swap(near_other, "group", 1), swap(far_other, "group", 1)]
    else:
        flip = jnp.int32(0)
        first, second = recompute_general(normed, w_kv, pair)
    holder_of = wanted // pass_local
    same = holder_of[:, None] == holder_of[None, :]
    before = jnp.arange(requests)[None, :] < jnp.arange(requests)[:, None]
    slot = holder_of * capacity + jnp.sum((same & before).astype(jnp.int32), axis=1)
    info = jnp.concatenate([jnp.stack([pair, flip]), slot]).astype(jnp.int32)
    other_info = jnp.concatenate([jnp.stack([1 - pair, flip]), slot]).astype(jnp.int32)
    out = attend(0, info, q_rows, own_kv, arrived, *first, bound)
    return attend(1, other_info, q_rows, own_kv, arrived, *second, bound, earlier=out)


def solution(mesh):
    rows = P(("group", "member"), None)
    placed = (
        rows,
        rows,
        P(("group", "member"), None, None),
        P(("group", "member"), None, None, None),
        P("member", "group"),
        rows,
        P(("group", "member"), None, None),
    )
    return jax.shard_map(local, mesh=mesh, in_specs=placed, out_specs=rows, check_vma=False)
```

profile of v0, /device:TPU:0, one launch (start us, length us, event | category | flops | bytes accessed | tf_op | source)
XLA Modules:
  0.0 123.6 jit_solution(8282389396986696038)
XLA Ops:
  0.0 3.0 %collective-permute-start.2 = (bf16[512,256]{1,0:T(8,128)(2,1)}, bf16[512,256]{1,0:T(8,128)(2,1)S(1)}, u32[]{:S(2)}, u32[]{:S(2)}) collective-permute-start(bf16[512,256]{1,0:T(8,128)(2,1)} %refs_0_.1), channel_id=1, source_target_pairs={{0,2},{1,3},{2,0},{3,1},{4,6},{5,7},{6,4},{7,5},{8,10},{9,11},{10,... | collective-permute-start | bytes 786440 | tf_op jit(solution)/shard_map/ppermute | solution.py:306
  3.0 2.6 %collective-permute-start.4 = (bf16[512,256]{1,0:T(8,128)(2,1)}, bf16[512,256]{1,0:T(8,128)(2,1)S(1)}, u32[]{:S(2)}, u32[]{:S(2)}) collective-permute-start(bf16[512,256]{1,0:T(8,128)(2,1)} %refs_0_.1), channel_id=1, source_target_pairs={{0,4},{1,5},{2,6},{3,7},{4,0},{5,1},{6,2},{7,3},{8,12},{9,13},{10,... | collective-permute-start | bytes 786440 | tf_op jit(solution)/shard_map/ppermute | solution.py:306
  5.6 1.5 %collective-permute-start = (bf16[512,256]{1,0:T(8,128)(2,1)}, bf16[512,256]{1,0:T(8,128)(2,1)S(1)}, u32[]{:S(2)}, u32[]{:S(2)}) collective-permute-start(bf16[512,256]{1,0:T(8,128)(2,1)} %refs_0_.1), channel_id=1, source_target_pairs={{0,1},{1,0},{2,3},{3,2},{4,5},{5,4},{6,7},{7,6},{8,9},{9,8},{10,11... | collective-permute-start | bytes 786440 | tf_op jit(solution)/shard_map/ppermute | solution.py:306
  7.1 1.5 %collective-permute-start.1 = (bf16[512,256]{1,0:T(8,128)(2,1)}, bf16[512,256]{1,0:T(8,128)(2,1)S(1)}, u32[]{:S(2)}, u32[]{:S(2)}) collective-permute-start(bf16[512,256]{1,0:T(8,128)(2,1)} %refs_0_.1), channel_id=1, source_target_pairs={{0,16},{8,24},{16,0},{24,8},{1,17},{9,25},{17,1},{25,9},{2,18},{10... | collective-permute-start | bytes 786440 | tf_op jit(solution)/shard_map/ppermute | solution.py:306
  8.6 0.8 reshape.79
  9.4 0.8 reshape.80
  10.2 4.9 %collective-permute-done.2.refs_2_ = bf16[512,256]{1,0:T(8,128)(2,1)S(1)} collective-permute-done((bf16[512,256]{1,0:T(8,128)(2,1)}, bf16[512,256]{1,0:T(8,128)(2,1)S(1)}, u32[]{:S(2)}, u32[]{:S(2)}) %collective-permute-start.2) | collective-permute-done | bytes 262176 | tf_op jit(solution)/shard_map/ppermute | solution.py:306
  15.0 1.7 %collective-permute-start.3 = (bf16[512,256]{1,0:T(8,128)(2,1)S(1)}, bf16[512,256]{1,0:T(8,128)(2,1)S(1)}, u32[]{:S(2)}, u32[]{:S(2)}) collective-permute-start(bf16[512,256]{1,0:T(8,128)(2,1)S(1)} %collective-permute-done.2.refs_2_), channel_id=1, source_target_pairs={{0,1},{1,0},{2,3},{3,2},{4,5},{5,4},{6,7},{7,6},{8,9},{9,8},{10,11... | collective-permute-start | bytes 786440 | tf_op jit(solution)/shard_map/ppermute | solution.py:306
  16.7 1.5 %collective-permute-start.6 = (bf16[512,256]{1,0:T(8,128)(2,1)S(1)}, bf16[512,256]{1,0:T(8,128)(2,1)S(1)}, u32[]{:S(2)}, u32[]{:S(2)}) collective-permute-start(bf16[512,256]{1,0:T(8,128)(2,1)S(1)} %collective-permute-done.2.refs_2_), channel_id=1, source_target_pairs={{0,16},{8,24},{16,0},{24,8},{1,17},{9,25},{17,1},{25,9},{2,18},{10... | collective-permute-start | bytes 786440 | tf_op jit(solution)/shard_map/ppermute | solution.py:306
  18.3 0.6 broadcast_in_dim.5
  18.9 4.6 %all-to-all-start = ((s32[8,3,128]{2,1,0:T(4,128)}), s32[8,3,128]{2,1,0:T(4,128)S(1)}, u32[]{:S(2)}, u32[]{:S(2)}) async-start(s32[8,3,128]{2,1,0:T(4,128)} %broadcast_in_dim.5), calls=%async_computation | async-start | bytes 32768 | tf_op jit(solution)/shard_map/all_to_all | solution.py:345
  23.5 0.6 pad_add_fusion.1.me_ref
  24.1 6.0 %all-to-all-done = s32[8,3,128]{2,1,0:T(4,128)S(1)} async-done(((s32[8,3,128]{2,1,0:T(4,128)}), s32[8,3,128]{2,1,0:T(4,128)S(1)}, u32[]{:S(2)}, u32[]{:S(2)}) %all-to-all-start) | async-done | bytes 12320 | tf_op jit(solution)/shard_map/all_to_all | solution.py:345
  30.1 0.6 reshape.81.table_ref
  30.7 4.1 %normalise.1.rest_0_.mine_ref = bf16[256,4096]{1,0:T(8,128)(2,1)} custom-call(bf16[256,4096]{1,0:T(8,128)(2,1)} %bitcast.10), custom_call_target="tpu_custom_call" | custom-call | flops 1 | bytes 1 | tf_op jit(solution)/shard_map/normalise/pallas_call | solution.py:44
  34.9 2.6 %find_rows.1 = (f32[16,64]{1,0:T(8,128)}, s32[16]{0:T(128)}) custom-call(s32[2]{0:T(128)} %pad_add_fusion.1.me_ref, s32[3072]{0:T(1024)} %reshape.81.table_ref), custom_call_target="tpu_custom_call" | custom-call | flops 1 | bytes 36000000 | tf_op jit(solution)/shard_map/find_rows/pallas_call | solution.py:90
  37.6 0.6 copy-done.2
  38.3 0.1 copy-done.6
  38.4 0.1 copy-done.4
  38.4 0.1 copy-done.9
  38.6 2.8 %pick_rows.1.refs_4_.rest_0_ = bf16[16,48,1024]{2,1,0:T(8,128)(2,1)} custom-call(s32[2]{0:T(128)} %pad_add_fusion.1.me_ref, s32[16]{0:T(128)} %get-tuple-element.11.passage_ref, f32[16,64]{1,0:T(8,128)} %get-tuple-element.12.rank_ref, bf16[4,64,1024]{2,1,0:T(8,128)(2,1)} %cache_ref.1, bf16[256,4096]{1,0:T(8,128)(2,1)} %normalise.1.rest_0_.mine_ref, ...), custom_call_target="tpu_custom_call" | custom-call | flops 1 | bytes 1 | tf_op jit(solution)/shard_map/pick_rows/pallas_call | solution.py:121
  41.4 4.6 %all-to-all-start.1 = ((bf16[8,96,1024]{2,1,0:T(8,128)(2,1)}), bf16[8,96,1024]{2,1,0:T(8,128)(2,1)}, u32[]{:S(2)}, u32[]{:S(2)}) async-start(bf16[8,96,1024]{2,1,0:T(8,128)(2,1)} %bitcast.9), calls=%async_computation.1 | async-start | bytes 3145728 | tf_op jit(solution)/shard_map/all_to_all | solution.py:355
  46.1 1.6 %collective-permute-start.11 = (bf16[512,256]{1,0:T(8,128)(2,1)S(1)}, bf16[512,256]{1,0:T(8,128)(2,1)S(1)}, u32[]{:S(2)}, u32[]{:S(2)}) collective-permute-start(bf16[512,256]{1,0:T(8,128)(2,1)S(1)} %copy-done.12), channel_id=1, source_target_pairs={{0,16},{8,24},{16,0},{24,8},{1,17},{9,25},{17,1},{25,9},{2,18},{10... | collective-permute-start | bytes 786440 | tf_op jit(solution)/shard_map/ppermute | solution.py:306
  47.7 0.5 collective-permute-start.10
  48.2 1.8 %collective-permute-start.8 = (bf16[512,256]{1,0:T(8,128)(2,1)S(1)}, bf16[512,256]{1,0:T(8,128)(2,1)S(1)}, u32[]{:S(2)}, u32[]{:S(2)}) collective-permute-start(bf16[512,256]{1,0:T(8,128)(2,1)S(1)} %copy-done.12), channel_id=1, source_target_pairs={{0,1},{1,0},{2,3},{3,2},{4,5},{5,4},{6,7},{7,6},{8,9},{9,8},{10,11... | collective-permute-start | bytes 786440 | tf_op jit(solution)/shard_map/ppermute | solution.py:306
  50.0 1.5 %collective-permute-start.13 = (bf16[512,256]{1,0:T(8,128)(2,1)S(1)}, bf16[512,256]{1,0:T(8,128)(2,1)S(1)}, u32[]{:S(2)}, u32[]{:S(2)}) collective-permute-start(bf16[512,256]{1,0:T(8,128)(2,1)S(1)} %copy-done.7), channel_id=1, source_target_pairs={{0,16},{8,24},{16,0},{24,8},{1,17},{9,25},{17,1},{25,9},{2,18},{10... | collective-permute-start | bytes 786440 | tf_op jit(solution)/shard_map/ppermute | solution.py:306
  51.5 3.7 %collective-permute-done.11.refs_3_ = bf16[512,256]{1,0:T(8,128)(2,1)S(1)} collective-permute-done((bf16[512,256]{1,0:T(8,128)(2,1)S(1)}, bf16[512,256]{1,0:T(8,128)(2,1)S(1)}, u32[]{:S(2)}, u32[]{:S(2)}) %collective-permute-start.11) | collective-permute-done | bytes 262176 | tf_op jit(solution)/shard_map/ppermute | solution.py:306
  55.3 1.8 %collective-permute-start.9 = (bf16[512,256]{1,0:T(8,128)(2,1)S(1)}, bf16[512,256]{1,0:T(8,128)(2,1)S(1)}, u32[]{:S(2)}, u32[]{:S(2)}) collective-permute-start(bf16[512,256]{1,0:T(8,128)(2,1)S(1)} %copy-done.7), channel_id=1, source_target_pairs={{0,1},{1,0},{2,3},{3,2},{4,5},{5,4},{6,7},{7,6},{8,9},{9,8},{10,11... | collective-permute-start | bytes 786440 | tf_op jit(solution)/shard_map/ppermute | solution.py:306
  57.1 3.8 %collective-permute-done.10.refs_2_ = bf16[512,256]{1,0:T(8,128)(2,1)S(1)} collective-permute-done((bf16[512,256]{1,0:T(8,128)(2,1)S(1)}, bf16[512,256]{1,0:T(8,128)(2,1)S(1)}, u32[]{:S(2)}, u32[]{:S(2)}) %collective-permute-start.10) | collective-permute-done | bytes 262176 | tf_op jit(solution)/shard_map/ppermute | solution.py:306
  60.9 1.5 %collective-permute-start.14 = (bf16[512,256]{1,0:T(8,128)(2,1)S(1)}, bf16[512,256]{1,0:T(8,128)(2,1)S(1)}, u32[]{:S(2)}, u32[]{:S(2)}) collective-permute-start(bf16[512,256]{1,0:T(8,128)(2,1)S(1)} %copy-done.5), channel_id=1, source_target_pairs={{0,16},{8,24},{16,0},{24,8},{1,17},{9,25},{17,1},{25,9},{2,18},{10... | collective-permute-start | bytes 786440 | tf_op jit(solution)/shard_map/ppermute | solution.py:306
  62.4 6.0 %collective-permute-done.8.refs_5_ = bf16[512,256]{1,0:T(8,128)(2,1)S(1)} collective-permute-done((bf16[512,256]{1,0:T(8,128)(2,1)S(1)}, bf16[512,256]{1,0:T(8,128)(2,1)S(1)}, u32[]{:S(2)}, u32[]{:S(2)}) %collective-permute-start.8) | collective-permute-done | bytes 262176 | tf_op jit(solution)/shard_map/ppermute | solution.py:306
  68.4 1.0 collective-permute-start.15
  69.4 0.2 convert_reduce_fusion
  69.7 1.3 %copy-done.1 = bf16[256,4096]{1,0:T(8,128)(2,1)} copy-done((bf16[256,4096]{1,0:T(8,128)(2,1)}, bf16[256,4096]{1,0:T(8,128)(2,1)S(1)}, u32[]{:S(2)}) %copy-start.1) | copy-done | bytes 2097176
  71.0 4.0 %project.3.refs_8_.refs_4_ = f32[512,256]{1,0:T(8,128)} custom-call(s32[1]{0:T(128)} %bitcast.2.member_ref, bf16[256,4096]{1,0:T(8,128)(2,1)} %normalise.1.rest_0_.mine_ref, bf16[256,4096]{1,0:T(8,128)(2,1)} %copy-done.1, bf16[512,256]{1,0:T(8,128)(2,1)} %copy-done.8, bf16[512,256]{1,0:T(8,128)(2,1)} %copy-done.9, bf16[512,256]{1,0:T(8,128)(2,1)} %copy-done.20, ...), custom_call_target="tpu_custom_call" | custom-call | flops 1 | bytes 18000000 | tf_op jit(solution)/shard_map/project/pallas_call | solution.py:157
  75.0 1.1 collective-permute-done.9.refs_7_
  76.1 0.7 copy-done.17
  76.8 4.7 %project.4 = (bf16[256,256]{1,0:T(8,128)(2,1)}, bf16[256,256]{1,0:T(8,128)(2,1)}) custom-call(s32[1]{0:T(128)} %bitcast.2.member_ref, bf16[256,4096]{1,0:T(8,128)(2,1)} %normalise.1.rest_0_.mine_ref, bf16[256,4096]{1,0:T(8,128)(2,1)} %copy-done.1, bf16[512,256]{1,0:T(8,128)(2,1)} %refs_0_.1, bf16[512,256]{1,0:T(8,128)(2,1)} %copy-done.2, ...), custom_call_target="tpu_custom_call" | custom-call | flops 1 | bytes 18000000 | tf_op jit(solution)/shard_map/project/pallas_call | solution.py:157
  81.5 0.7 copy-done.15
  82.2 0.1 copy-done.16
  82.3 0.1 copy-done.18
  82.4 4.0 %project.5 = (bf16[256,256]{1,0:T(8,128)(2,1)}, bf16[256,256]{1,0:T(8,128)(2,1)}) custom-call(s32[1]{0:T(128)} %bitcast.2.member_ref, bf16[256,4096]{1,0:T(8,128)(2,1)} %normalise.1.rest_0_.mine_ref, bf16[256,4096]{1,0:T(8,128)(2,1)} %copy-done.1, bf16[512,256]{1,0:T(8,128)(2,1)} %copy-done.13, bf16[512,256]{1,0:T(8,128)(2,1)} %copy-done.15, ...), custom_call_target="tpu_custom_call" | custom-call | flops 1 | bytes 18000000 | tf_op jit(solution)/shard_map/project/pallas_call | solution.py:157
  86.4 0.5 collective-permute-start.12
  87.0 0.6 add_add_fusion.1
  87.6 4.1 %query_bound.1.bound_ref = f32[8,128]{1,0:T(8,128)} custom-call(bf16[256,8192]{1,0:T(8,128)(2,1)} %q_ref.5, bf16[16,48,1024]{2,1,0:T(8,128)(2,1)} %pick_rows.1.refs_4_.rest_0_), custom_call_target="tpu_custom_call" | custom-call | flops 1 | bytes 1 | tf_op jit(solution)/shard_map/query_bound/pallas_call | solution.py:189
  91.7 15.5 %attend.2.rest_0_ = bf16[256,8192]{1,0:T(8,128)(2,1)} custom-call(s32[18]{0:T(128)} %get-tuple-element.17.info_ref, bf16[256,8192]{1,0:T(8,128)(2,1)} %q_ref.5, bf16[256,1024]{1,0:T(8,128)(2,1)} %own_v_ref.3, bf16[256,1024]{1,0:T(8,128)(2,1)} %own_v_ref.3, bf16[16,48,1024]{2,1,0:T(8,128)(2,1)} %bitcast.7.kept_ref, ...), custom_call_target="tpu_custom_call" | custom-call | flops 1 | bytes 1 | tf_op jit(solution)/shard_map/attend/pallas_call | solution.py:283
  107.2 0.6 copy-done.21
  107.9 15.7 %attend.3 = bf16[256,8192]{1,0:T(8,128)(2,1)} custom-call(s32[18]{0:T(128)} %get-tuple-element.18.info_ref, bf16[256,8192]{1,0:T(8,128)(2,1)} %q_ref.5, bf16[256,1024]{1,0:T(8,128)(2,1)} %own_v_ref.3, bf16[256,1024]{1,0:T(8,128)(2,1)} %own_v_ref.3, bf16[16,48,1024]{2,1,0:T(8,128)(2,1)} %bitcast.7.kept_ref, ...), custom_call_target="tpu_custom_call", output_to_operand_aliasing={{}: (8, {})} | custom-call | flops 1 | bytes 1 | tf_op jit(solution)/shard_map/attend/pallas_call | solution.py:283
  (60 shorter events, 0.4 us)
Async XLA Ops:
  0.0 15.0 %collective-permute-start.2 = (bf16[512,256]{1,0:T(8,128)(2,1)}, bf16[512,256]{1,0:T(8,128)(2,1)S(1)}, u32[]{:S(2)}, u32[]{:S(2)}) collective-permute-start(bf16[512,256]{1,0:T(8,128)(2,1)} %refs_0_.1), channel_id=1, source_target_pairs={{0,2},{1,3},{2,0},{3,1},{4,6},{5,7},{6,4},{7,5},{8,10},{9,11},{10,... | collective-permute-start | bytes 786440 | tf_op jit(solution)/shard_map/ppermute | solution.py:306
  3.0 15.2 %collective-permute-start.4 = (bf16[512,256]{1,0:T(8,128)(2,1)}, bf16[512,256]{1,0:T(8,128)(2,1)S(1)}, u32[]{:S(2)}, u32[]{:S(2)}) collective-permute-start(bf16[512,256]{1,0:T(8,128)(2,1)} %refs_0_.1), channel_id=1, source_target_pairs={{0,4},{1,5},{2,6},{3,7},{4,0},{5,1},{6,2},{7,3},{8,12},{9,13},{10,... | collective-permute-start | bytes 786440 | tf_op jit(solution)/shard_map/ppermute | solution.py:306
  5.6 31.9 %collective-permute-start = (bf16[512,256]{1,0:T(8,128)(2,1)}, bf16[512,256]{1,0:T(8,128)(2,1)S(1)}, u32[]{:S(2)}, u32[]{:S(2)}) collective-permute-start(bf16[512,256]{1,0:T(8,128)(2,1)} %refs_0_.1), channel_id=1, source_target_pairs={{0,1},{1,0},{2,3},{3,2},{4,5},{5,4},{6,7},{7,6},{8,9},{9,8},{10,11... | collective-permute-start | bytes 786440 | tf_op jit(solution)/shard_map/ppermute | solution.py:306
  7.1 30.4 %collective-permute-start.1 = (bf16[512,256]{1,0:T(8,128)(2,1)}, bf16[512,256]{1,0:T(8,128)(2,1)S(1)}, u32[]{:S(2)}, u32[]{:S(2)}) collective-permute-start(bf16[512,256]{1,0:T(8,128)(2,1)} %refs_0_.1), channel_id=1, source_target_pairs={{0,16},{8,24},{16,0},{24,8},{1,17},{9,25},{17,1},{25,9},{2,18},{10... | collective-permute-start | bytes 786440 | tf_op jit(solution)/shard_map/ppermute | solution.py:306
  15.0 19.8 %copy-start.10 = (bf16[512,256]{1,0:T(8,128)(2,1)}, bf16[512,256]{1,0:T(8,128)(2,1)S(1)}, u32[]{:S(2)}) copy-start(bf16[512,256]{1,0:T(8,128)(2,1)S(1)} %collective-permute-done.2.refs_2_) | copy-start | bytes 786436
  15.0 22.5 %collective-permute-start.3 = (bf16[512,256]{1,0:T(8,128)(2,1)S(1)}, bf16[512,256]{1,0:T(8,128)(2,1)S(1)}, u32[]{:S(2)}, u32[]{:S(2)}) collective-permute-start(bf16[512,256]{1,0:T(8,128)(2,1)S(1)} %collective-permute-done.2.refs_2_), channel_id=1, source_target_pairs={{0,1},{1,0},{2,3},{3,2},{4,5},{5,4},{6,7},{7,6},{8,9},{9,8},{10,11... | collective-permute-start | bytes 786440 | tf_op jit(solution)/shard_map/ppermute | solution.py:306
  16.7 20.8 %collective-permute-start.6 = (bf16[512,256]{1,0:T(8,128)(2,1)S(1)}, bf16[512,256]{1,0:T(8,128)(2,1)S(1)}, u32[]{:S(2)}, u32[]{:S(2)}) collective-permute-start(bf16[512,256]{1,0:T(8,128)(2,1)S(1)} %collective-permute-done.2.refs_2_), channel_id=1, source_target_pairs={{0,16},{8,24},{16,0},{24,8},{1,17},{9,25},{17,1},{25,9},{2,18},{10... | collective-permute-start | bytes 786440 | tf_op jit(solution)/shard_map/ppermute | solution.py:306
  18.2 16.6 %copy-start.11 = (bf16[512,256]{1,0:T(8,128)(2,1)}, bf16[512,256]{1,0:T(8,128)(2,1)S(1)}, u32[]{:S(2)}) copy-start(bf16[512,256]{1,0:T(8,128)(2,1)S(1)} %collective-permute-done.4.refs_4_) | copy-start | bytes 786436
  18.2 19.3 %collective-permute-start.5 = (bf16[512,256]{1,0:T(8,128)(2,1)S(1)}, bf16[512,256]{1,0:T(8,128)(2,1)S(1)}, u32[]{:S(2)}, u32[]{:S(2)}) collective-permute-start(bf16[512,256]{1,0:T(8,128)(2,1)S(1)} %collective-permute-done.4.refs_4_), channel_id=1, source_target_pairs={{0,2},{1,3},{2,0},{3,1},{4,6},{5,7},{6,4},{7,5},{8,10},{9,11},{10,... | collective-permute-start | bytes 786440 | tf_op jit(solution)/shard_map/ppermute | solution.py:306
  18.9 11.2 %all-to-all-start = ((s32[8,3,128]{2,1,0:T(4,128)}), s32[8,3,128]{2,1,0:T(4,128)S(1)}, u32[]{:S(2)}, u32[]{:S(2)}) async-start(s32[8,3,128]{2,1,0:T(4,128)} %broadcast_in_dim.5), calls=%async_computation | async-start | bytes 32768 | tf_op jit(solution)/shard_map/all_to_all | solution.py:345
  37.5 0.7 copy-start.2
  37.5 0.8 copy-start.8
  37.5 0.8 copy-start.6
  37.5 0.9 copy-start.4
  37.6 1.0 copy-start.9
  41.4 4.6 %copy-start = (bf16[256,4096]{1,0:T(8,128)(2,1)S(1)}, bf16[256,4096]{1,0:T(8,128)(2,1)}, u32[]{:S(2)}) copy-start(bf16[256,4096]{1,0:T(8,128)(2,1)} %normalise.1.rest_0_.mine_ref) | copy-start | bytes 6291460
  41.4 4.7 %copy-start.12 = (bf16[512,256]{1,0:T(8,128)(2,1)S(1)}, bf16[512,256]{1,0:T(8,128)(2,1)}, u32[]{:S(2)}) copy-start(bf16[512,256]{1,0:T(8,128)(2,1)} %copy-done.11) | copy-start | bytes 786436
  41.4 6.3 %copy-start.3 = (bf16[512,256]{1,0:T(8,128)(2,1)S(1)}, bf16[512,256]{1,0:T(8,128)(2,1)}, u32[]{:S(2)}) copy-start(bf16[512,256]{1,0:T(8,128)(2,1)} %copy-done.2) | copy-start | bytes 786436
  41.4 8.6 %copy-start.7 = (bf16[512,256]{1,0:T(8,128)(2,1)S(1)}, bf16[512,256]{1,0:T(8,128)(2,1)}, u32[]{:S(2)}) copy-start(bf16[512,256]{1,0:T(8,128)(2,1)} %copy-done.6) | copy-start | bytes 786436
  41.4 19.5 %copy-start.5 = (bf16[512,256]{1,0:T(8,128)(2,1)S(1)}, bf16[512,256]{1,0:T(8,128)(2,1)}, u32[]{:S(2)}) copy-start(bf16[512,256]{1,0:T(8,128)(2,1)} %copy-done.4) | copy-start | bytes 786436
  41.4 50.3 %all-to-all-start.1 = ((bf16[8,96,1024]{2,1,0:T(8,128)(2,1)}), bf16[8,96,1024]{2,1,0:T(8,128)(2,1)}, u32[]{:S(2)}, u32[]{:S(2)}) async-start(bf16[8,96,1024]{2,1,0:T(8,128)(2,1)} %bitcast.9), calls=%async_computation.1 | async-start | bytes 3145728 | tf_op jit(solution)/shard_map/all_to_all | solution.py:355
  46.0 23.6 %collective-permute-start.7 = (bf16[256,4096]{1,0:T(8,128)(2,1)S(1)}, bf16[256,4096]{1,0:T(8,128)(2,1)S(1)}, u32[]{:S(2)}, u32[]{:S(2)}) collective-permute-start(bf16[256,4096]{1,0:T(8,128)(2,1)S(1)} %copy-done), channel_id=1, source_target_pairs={{0,8},{8,0},{16,24},{24,16},{1,9},{9,1},{17,25},{25,17},{2,10},{10... | collective-permute-start | bytes 6291464 | tf_op jit(solution)/shard_map/ppermute | solution.py:306
  46.1 9.2 %collective-permute-start.11 = (bf16[512,256]{1,0:T(8,128)(2,1)S(1)}, bf16[512,256]{1,0:T(8,128)(2,1)S(1)}, u32[]{:S(2)}, u32[]{:S(2)}) collective-permute-start(bf16[512,256]{1,0:T(8,128)(2,1)S(1)} %copy-done.12), channel_id=1, source_target_pairs={{0,16},{8,24},{16,0},{24,8},{1,17},{9,25},{17,1},{25,9},{2,18},{10... | collective-permute-start | bytes 786440 | tf_op jit(solution)/shard_map/ppermute | solution.py:306
  47.7 13.2 %collective-permute-start.10 = (bf16[512,256]{1,0:T(8,128)(2,1)S(1)}, bf16[512,256]{1,0:T(8,128)(2,1)S(1)}, u32[]{:S(2)}, u32[]{:S(2)}) collective-permute-start(bf16[512,256]{1,0:T(8,128)(2,1)S(1)} %copy-done.3), channel_id=1, source_target_pairs={{0,16},{8,24},{16,0},{24,8},{1,17},{9,25},{17,1},{25,9},{2,18},{10... | collective-permute-start | bytes 786440 | tf_op jit(solution)/shard_map/ppermute | solution.py:306
  48.2 20.2 %collective-permute-start.8 = (bf16[512,256]{1,0:T(8,128)(2,1)S(1)}, bf16[512,256]{1,0:T(8,128)(2,1)S(1)}, u32[]{:S(2)}, u32[]{:S(2)}) collective-permute-start(bf16[512,256]{1,0:T(8,128)(2,1)S(1)} %copy-done.12), channel_id=1, source_target_pairs={{0,1},{1,0},{2,3},{3,2},{4,5},{5,4},{6,7},{7,6},{8,9},{9,8},{10,11... | collective-permute-start | bytes 786440 | tf_op jit(solution)/shard_map/ppermute | solution.py:306
  50.0 19.4 %collective-permute-start.13 = (bf16[512,256]{1,0:T(8,128)(2,1)S(1)}, bf16[512,256]{1,0:T(8,128)(2,1)S(1)}, u32[]{:S(2)}, u32[]{:S(2)}) collective-permute-start(bf16[512,256]{1,0:T(8,128)(2,1)S(1)} %copy-done.7), channel_id=1, source_target_pairs={{0,16},{8,24},{16,0},{24,8},{1,17},{9,25},{17,1},{25,9},{2,18},{10... | collective-permute-start | bytes 786440 | tf_op jit(solution)/shard_map/ppermute | solution.py:306
  55.3 14.4 %copy-start.19 = (bf16[512,256]{1,0:T(8,128)(2,1)}, bf16[512,256]{1,0:T(8,128)(2,1)S(1)}, u32[]{:S(2)}) copy-start(bf16[512,256]{1,0:T(8,128)(2,1)S(1)} %collective-permute-done.11.refs_3_) | copy-start | bytes 786436
  55.3 20.8 %collective-permute-start.9 = (bf16[512,256]{1,0:T(8,128)(2,1)S(1)}, bf16[512,256]{1,0:T(8,128)(2,1)S(1)}, u32[]{:S(2)}, u32[]{:S(2)}) collective-permute-start(bf16[512,256]{1,0:T(8,128)(2,1)S(1)} %copy-done.7), channel_id=1, source_target_pairs={{0,1},{1,0},{2,3},{3,2},{4,5},{5,4},{6,7},{7,6},{8,9},{9,8},{10,11... | collective-permute-start | bytes 786440 | tf_op jit(solution)/shard_map/ppermute | solution.py:306
  60.9 8.7 %copy-start.20 = (bf16[512,256]{1,0:T(8,128)(2,1)}, bf16[512,256]{1,0:T(8,128)(2,1)S(1)}, u32[]{:S(2)}) copy-start(bf16[512,256]{1,0:T(8,128)(2,1)S(1)} %collective-permute-done.10.refs_2_) | copy-start | bytes 786436
  60.9 20.6 %collective-permute-start.14 = (bf16[512,256]{1,0:T(8,128)(2,1)S(1)}, bf16[512,256]{1,0:T(8,128)(2,1)S(1)}, u32[]{:S(2)}, u32[]{:S(2)}) collective-permute-start(bf16[512,256]{1,0:T(8,128)(2,1)S(1)} %copy-done.5), channel_id=1, source_target_pairs={{0,16},{8,24},{16,0},{24,8},{1,17},{9,25},{17,1},{25,9},{2,18},{10... | collective-permute-start | bytes 786440 | tf_op jit(solution)/shard_map/ppermute | solution.py:306
  68.4 7.7 %copy-start.14 = (bf16[512,256]{1,0:T(8,128)(2,1)}, bf16[512,256]{1,0:T(8,128)(2,1)S(1)}, u32[]{:S(2)}) copy-start(bf16[512,256]{1,0:T(8,128)(2,1)S(1)} %collective-permute-done.8.refs_5_) | copy-start | bytes 786436
  68.4 13.1 %collective-permute-start.15 = (bf16[512,256]{1,0:T(8,128)(2,1)S(1)}, bf16[512,256]{1,0:T(8,128)(2,1)S(1)}, u32[]{:S(2)}, u32[]{:S(2)}) collective-permute-start(bf16[512,256]{1,0:T(8,128)(2,1)S(1)} %collective-permute-done.8.refs_5_), channel_id=1, source_target_pairs={{0,16},{8,24},{16,0},{24,8},{1,17},{9,25},{17,1},{25,9},{2,18},{10... | collective-permute-start | bytes 786440 | tf_op jit(solution)/shard_map/ppermute | solution.py:306
  69.4 12.1 %copy-start.13 = (bf16[512,256]{1,0:T(8,128)(2,1)}, bf16[512,256]{1,0:T(8,128)(2,1)S(1)}, u32[]{:S(2)}) copy-start(bf16[512,256]{1,0:T(8,128)(2,1)S(1)} %collective-permute-done.13.refs_0_) | copy-start | bytes 786436
  69.4 12.1 %collective-permute-start.16 = (bf16[512,256]{1,0:T(8,128)(2,1)S(1)}, bf16[512,256]{1,0:T(8,128)(2,1)S(1)}, u32[]{:S(2)}, u32[]{:S(2)}) collective-permute-start(bf16[512,256]{1,0:T(8,128)(2,1)S(1)} %collective-permute-done.13.refs_0_), channel_id=1, source_target_pairs={{0,1},{1,0},{2,3},{3,2},{4,5},{5,4},{6,7},{7,6},{8,9},{9,8},{10,11... | collective-permute-start | bytes 786440 | tf_op jit(solution)/shard_map/ppermute | solution.py:306
  69.6 1.3 %copy-start.1 = (bf16[256,4096]{1,0:T(8,128)(2,1)}, bf16[256,4096]{1,0:T(8,128)(2,1)S(1)}, u32[]{:S(2)}) copy-start(bf16[256,4096]{1,0:T(8,128)(2,1)S(1)} %collective-permute-done.7.other_ref) | copy-start | bytes 6291460
  76.1 0.7 copy-start.17
  81.5 0.7 copy-start.15
  81.5 0.8 copy-start.16
  81.5 0.9 copy-start.18
  82.4 4.0 %copy-start.23 = (bf16[256,256]{1,0:T(8,128)(2,1)S(1)}, bf16[256,256]{1,0:T(8,128)(2,1)}, u32[]{:S(2)}) copy-start(bf16[256,256]{1,0:T(8,128)(2,1)} %get-tuple-element.13) | copy-start | bytes 393220
  86.4 20.8 %collective-permute-start.17 = (bf16[256,256]{1,0:T(8,128)(2,1)}, bf16[256,256]{1,0:T(8,128)(2,1)S(1)}, u32[]{:S(2)}, u32[]{:S(2)}) collective-permute-start(bf16[256,256]{1,0:T(8,128)(2,1)} %get-tuple-element.15), channel_id=1, source_target_pairs={{0,8},{8,0},{16,24},{24,16},{1,9},{9,1},{17,25},{25,17},{2,10},{10... | collective-permute-start | bytes 393224 | tf_op jit(solution)/shard_map/ppermute | solution.py:306
  86.4 20.8 %collective-permute-start.12 = (bf16[256,256]{1,0:T(8,128)(2,1)S(1)}, bf16[256,256]{1,0:T(8,128)(2,1)S(1)}, u32[]{:S(2)}, u32[]{:S(2)}) collective-permute-start(bf16[256,256]{1,0:T(8,128)(2,1)S(1)} %copy-done.23), channel_id=1, source_target_pairs={{0,8},{8,0},{16,24},{24,16},{1,9},{9,1},{17,25},{25,17},{2,10},{10... | collective-permute-start | bytes 393224 | tf_op jit(solution)/shard_map/ppermute | solution.py:306
  107.2 0.7 copy-start.21
  107.2 0.7 copy-start.22
where the time goes:
time: 125 us; the launch traced here: 124 us
  Pallas kernels  57.5 us (46%)
  starting transfers between devices  31.4 us (25%)
  waiting for transfers between devices  25.5 us (20%)
  local copies, waits for them, and re-layouts  7.42 us (6%)
  other arithmetic  1.5 us (1%)
    pallas_call x2, Pallas kernels, attend(): pl.pallas_call(functools.partial(attend_kernel, 8), grid_spec=pltpu.Prefe...  31.2 us
    ppermute x18, starting transfers between devices, swap(): return lax.ppermute(array, axis, [(i, i ^ bits) for i in range(size)])  22.2 us
    ppermute x18, waiting for transfers between devices, swap(): return lax.ppermute(array, axis, [(i, i ^ bits) for i in range(size)])  19.5 us
    pallas_call x3, Pallas kernels, project(): pl.pallas_call(functools.partial(project_kernel, len(weights), wanted, bo...  12.7 us
    all_to_all x1, waiting for transfers between devices, local(): lax.all_to_all(request, 'member', split_axis=0, concat_axis=0, tiled=True)  5.97 us
    unnamed x48, local copies, waits for them, and re-layouts  4.64 us
    all_to_all x1, starting transfers between devices, local(): lax.all_to_all(request, 'member', split_axis=0, concat_axis=0, tiled=True)  4.6 us
    all_to_all x1, starting transfers between devices, local(): lax.all_to_all(sent.reshape(holders, capacity * KEPT, 2 * HALF), 'member'...  4.57 us
  transfers between devices with their start and end apart: 20, of which 6 were waited for; matrix products, arithmetic and copies ran while one was open for 3% of the time, Pallas kernels for 32%

commit v1 on v0

--- a/solution.py
+++ b/solution.py
@@ -53,7 +53,9 @@
     )(hidden, *ahead)
 
 
-def find_kernel(holders, requests, pass_local, capacity, me_ref, table_ref, rank_ref, passage_ref, slot_ref, kept_ref):
+def find_kernel(holders, requests, pass_local, capacity, passing, me_ref, table_ref, *rest):
+    rank_ref, passage_ref = rest[passing : passing + 2]
+    slot_ref, kept_ref = rest[-2:]
     me = me_ref[0]
     stride = table_ref.shape[0] // holders
     for k in range(holders):
@@ -84,19 +86,22 @@
     rank_ref[...] = jnp.where(kept > 0, rank_of, 0.0)
 
 
-def find_rows(table, me, holders, requests, pass_local, capacity):
+def find_rows(table, me, holders, requests, pass_local, capacity, passing):
     slots = holders * capacity
     smem = pl.BlockSpec(memory_space=pltpu.SMEM)
-    return pl.pallas_call(
-        functools.partial(find_kernel, holders, requests, pass_local, capacity),
-        in_specs=[smem, smem],
-        out_specs=[pl.BlockSpec(memory_space=pltpu.VMEM), smem],
-        out_shape=[jax.ShapeDtypeStruct((slots, PLEN), jnp.float32), jax.ShapeDtypeStruct((slots,), jnp.int32)],
+    whole = pl.BlockSpec(memory_space=pl.ANY)
+    return pl.pallas_call(
+        functools.partial(find_kernel, holders, requests, pass_local, capacity, len(passing)),
+        in_specs=[smem, smem] + [whole] * len(passing),
+        out_specs=[pl.BlockSpec(memory_space=pltpu.VMEM), smem] + [whole] * len(passing),
+        out_shape=[jax.ShapeDtypeStruct((slots, PLEN), jnp.float32), jax.ShapeDtypeStruct((slots,), jnp.int32)]
+        + [jax.ShapeDtypeStruct(part.shape, part.dtype) for part in passing],
+        input_output_aliases={2 + i: 2 + i for i in range(len(passing))},
         scratch_shapes=[pltpu.SMEM((holders * (capacity + 1),), jnp.int32), pltpu.VMEM((slots, PLEN), jnp.float32)],
         compiler_params=pltpu.CompilerParams(vmem_limit_bytes=VMEM_BYTES),
         cost_estimate=LARGE,
         name="find_rows",
-    )(me, table)
+    )(me, table, *passing)
 
 
 def pick_kernel(me_ref, passage_ref, rank_ref, cache_ref, *rest):
@@ -167,40 +172,104 @@
     )(member.reshape(1), mine, other, *[weights[k] for k in wanted], *carried, *ahead)
 
 
-def bound_kernel(q_ref, *rest):
-    bound_ref = rest[-1]
-
-    @pl.when(pl.program_id(0) == 0)
+def scaled_keys(keys, turned_ref):
+    scaled = keys.astype(jnp.float32) * SCORE_FACTOR
+    high = scaled.astype(jnp.bfloat16)
+    turned_ref[:HD, :] = high.T
+    turned_ref[HD:, :] = (scaled - high.astype(jnp.float32)).astype(jnp.bfloat16).T
+    return jnp.max(jnp.sum(scaled * scaled, axis=1, keepdims=True))
+
+
+def head_rows(q_ref, first, heads_once):
+    block = jnp.concatenate(
+        [q_ref[:, (first + i) * HD : (first + i + 1) * HD] for i in range(heads_once)], axis=0
+    )
+    return jnp.concatenate([block, block], axis=1)
+
+
+def causal(rows):
+    token = lax.broadcasted_iota(jnp.int32, (rows, QLEN), 0) % QLEN
+    return lax.broadcasted_iota(jnp.int32, (rows, QLEN), 1) <= token
+
+
+def own_kernel(heads_once, info_ref, q_ref, key_ref, value_ref, *rest):
+    sum_ref, weight_ref, bound_ref, turned_ref, wide_ref = rest[-5:]
+
+    @pl.when((pl.program_id(0) == 0) & (pl.program_id(1) == 0))
     def clear():
         bound_ref[...] = jnp.zeros_like(bound_ref)
 
-    peak = jnp.zeros((q_ref.shape[0], 1), jnp.float32)
-    for first in range(0, GROUPED, 4):
-        most = None
-        for head in range(first, first + 4):
-            block = q_ref[:, head * HD : (head + 1) * HD].astype(jnp.float32)
-            most = block * block if most is None else jnp.maximum(most, block * block)
-        peak = jnp.maximum(peak, jnp.sum(most, axis=1, keepdims=True))
+    scaled_keys(key_ref[...], turned_ref)
+    wide_ref[:, :HD] = value_ref[...]
+    wide_ref[:, HD:] = jnp.ones((QLEN, HD), jnp.bfloat16)
+    shown = jnp.where(causal(heads_once * QLEN), 1.0, 0.0).astype(jnp.bfloat16)
+    lane = lax.broadcasted_iota(jnp.int32, (QLEN, HD), 1)
+    weights = jnp.zeros((QLEN, HD), jnp.float32)
+    peak = jnp.zeros((QLEN, 1), jnp.float32)
+    for first in range(0, GROUPED, heads_once):
+        scores = jnp.dot(head_rows(q_ref, first, heads_once), turned_ref[...], preferred_element_type=jnp.float32)
+        summed = jnp.dot(
+            jnp.exp2(scores).astype(jnp.bfloat16) * shown, wide_ref[...], preferred_element_type=jnp.float32
+        )
+        for i in range(heads_once):
+            rows = slice(i * QLEN, (i + 1) * QLEN)
+            sum_ref[:, (first + i) * HD : (first + i + 1) * HD] = summed[rows, :HD].astype(jnp.bfloat16)
+            weights = jnp.where(lane == first + i, summed[rows, HD:], weights)
+        for pair in range(first, first + heads_once, 4):
+            most = None
+            for head in range(pair, pair + 4):
+                block = q_ref[:, head * HD : (head + 1) * HD].astype(jnp.float32)
+                most = block * block if most is None else jnp.maximum(most, block * block)
+            peak = jnp.maximum(peak, jnp.sum(most, axis=1, keepdims=True))
+    weight_ref[...] = weights
     bound_ref[...] = jnp.maximum(bound_ref[...], jnp.max(peak))
 
 
-def query_bound(q_rows, ahead):
-    rows, width = q_rows.shape
-    return pl.pallas_call(
-        bound_kernel,
-        grid=(KVH,),
-        in_specs=[pl.BlockSpec((rows, GROUPED * HD), lambda h: (0, h))]
-        + [pl.BlockSpec(memory_space=pl.ANY)] * len(ahead),
-        out_specs=pl.BlockSpec((8, HD), lambda h: (0, 0)),
-        out_shape=jax.ShapeDtypeStruct((8, HD), jnp.float32),
+def attend_own(info, q_rows, own_kv, ahead):
+    rows = q_rows.shape[0]
+    wide = GROUPED * HD
+    return pl.pallas_call(
+        functools.partial(own_kernel, 8),
+        grid_spec=pltpu.PrefetchScalarGridSpec(
+            num_scalar_prefetch=1,
+            grid=(rows // QLEN, PAIR_HEADS),
+            in_specs=[
+                pl.BlockSpec((QLEN, wide), lambda n, h, info: (n, info[0] * PAIR_HEADS + h)),
+                pl.BlockSpec((QLEN, HD), lambda n, h, info: (n, info[0] * PAIR_HEADS + h)),
+                pl.BlockSpec((QLEN, HD), lambda n, h, info: (n, KVH + info[0] * PAIR_HEADS + h)),
+            ]
+            + [pl.BlockSpec(memory_space=pl.ANY)] * len(ahead),
+            out_specs=[
+                pl.BlockSpec((QLEN, wide), lambda n, h, info: (n, h)),
+                pl.BlockSpec((QLEN, HD), lambda n, h, info: (n, h)),
+                pl.BlockSpec((8, HD), lambda n, h, info: (0, 0)),
+            ],
+            scratch_shapes=[pltpu.VMEM((2 * HD, QLEN), jnp.bfloat16), pltpu.VMEM((QLEN, 2 * HD), jnp.bfloat16)],
+        ),
+        out_shape=[
+            jax.ShapeDtypeStruct((rows, PAIR_HEADS * wide), jnp.bfloat16),
+            jax.ShapeDtypeStruct((rows, PAIR_HEADS * HD), jnp.float32),
+            jax.ShapeDtypeStruct((8, HD), jnp.float32),
+        ],
         compiler_params=pltpu.CompilerParams(vmem_limit_bytes=VMEM_BYTES),
         cost_estimate=LITTLE,
-        name="query_bound",
-    )(q_rows, *ahead)
+        name="attend_own",
+    )(info, q_rows, own_kv, own_kv, *ahead)
 
 
 def attend_kernel(
-    heads_once, info_ref, q_ref, own_k_ref, own_v_ref, kept_ref, near_ref, far_ref, bound_ref, *rest
+    heads_once,
+    info_ref,
+    q_ref,
+    own_k_ref,
+    own_v_ref,
+    kept_ref,
+    near_ref,
+    far_ref,
+    sum_ref,
+    weight_ref,
+    bound_ref,
+    *rest,
 ):
     out_ref, key_ref, turned_ref, value_ref = rest[-4:]
     query = pl.program_id(0)
@@ -217,49 +286,49 @@
     value_ref[TOPP * KEPT : passage_keys, :HD] = jnp.where(flip, near_ref[...], far_ref[...])
     key_ref[passage_keys:, :] = own_k_ref[...]
     value_ref[passage_keys:, :HD] = own_v_ref[...]
-    scaled = key_ref[...].astype(jnp.float32) * SCORE_FACTOR
-    high = scaled.astype(jnp.bfloat16)
-    turned_ref[:HD, :] = high.T
-    turned_ref[HD:, :] = (scaled - high.astype(jnp.float32)).astype(jnp.bfloat16).T
-    key_bound = jnp.max(jnp.sum(scaled * scaled, axis=1, keepdims=True))
+    key_bound = scaled_keys(key_ref[...], turned_ref)
     small = jnp.max(bound_ref[...]) * key_bound <= SAFE_EXPONENT**2
     rows = heads_once * QLEN
-    token = lax.broadcasted_iota(jnp.int32, (rows, QLEN), 0) % QLEN
-    visible = lax.broadcasted_iota(jnp.int32, (rows, QLEN), 1) <= token
-
-    def score(first):
-        block = jnp.concatenate(
-            [q_ref[:, (first + i) * HD : (first + i + 1) * HD] for i in range(heads_once)], axis=0
-        )
-        return jnp.dot(
-            jnp.concatenate([block, block], axis=1), turned_ref[...], preferred_element_type=jnp.float32
-        )
-
-    def store(first, expd):
-        summed = jnp.dot(expd, value_ref[...], preferred_element_type=jnp.float32)
-        result = (summed[:, :HD] / summed[:, HD:]).astype(jnp.bfloat16)
-        for i in range(heads_once):
-            out_ref[:, (first + i) * HD : (first + i + 1) * HD] = result[i * QLEN : (i + 1) * QLEN]
 
     @pl.when(small)
     def unshifted():
-        shown = jnp.where(visible, 1.0, 0.0).astype(jnp.bfloat16)
         for first in range(0, GROUPED, heads_once):
-            expd = jnp.exp2(score(first)).astype(jnp.bfloat16)
-            store(first, jnp.concatenate([expd[:, :passage_keys], expd[:, passage_keys:] * shown], axis=1))
+            scores = jnp.dot(
+                head_rows(q_ref, first, heads_once),
+                turned_ref[:, :passage_keys],
+                preferred_element_type=jnp.float32,
+            )
+            summed = jnp.dot(
+                jnp.exp2(scores).astype(jnp.bfloat16),
+                value_ref[:passage_keys, :],
+                preferred_element_type=jnp.float32,
+            )
+            for i in range(heads_once):
+                part = summed[i * QLEN : (i + 1) * QLEN]
+                columns = slice((first + i) * HD, (first + i + 1) * HD)
+                total = part[:, :HD] + sum_ref[:, columns].astype(jnp.float32)
+                weight = part[:, HD:] + weight_ref[:, first + i : first + i + 1]
+                out_ref[:, columns] = (total / weight).astype(jnp.bfloat16)
 
     @pl.when(jnp.logical_not(small))
     def shifted():
+        visible = causal(rows)
         for first in range(0, GROUPED, heads_once):
-            scores = score(first)
+            scores = jnp.dot(
+                head_rows(q_ref, first, heads_once), turned_ref[...], preferred_element_type=jnp.float32
+            )
             scores = jnp.concatenate(
                 [scores[:, :passage_keys], jnp.where(visible, scores[:, passage_keys:], -jnp.inf)], axis=1
             )
             peak = jnp.max(scores, axis=1, keepdims=True)
-            store(first, jnp.exp2(scores - peak).astype(jnp.bfloat16))
-
-
-def attend(part, info, q_rows, own_kv, kept, near, far, bound, earlier=None):
+            expd = jnp.exp2(scores - peak).astype(jnp.bfloat16)
+            summed = jnp.dot(expd, value_ref[...], preferred_element_type=jnp.float32)
+            result = (summed[:, :HD] / summed[:, HD:]).astype(jnp.bfloat16)
+            for i in range(heads_once):
+                out_ref[:, (first + i) * HD : (first + i + 1) * HD] = result[i * QLEN : (i + 1) * QLEN]
+
+
+def attend(part, info, q_rows, own_kv, kept, near, far, own, earlier=None):
     rows, width = q_rows.shape
     queries = rows // QLEN
     slots = kept.shape[0]
@@ -272,9 +341,11 @@
         pl.BlockSpec((slots, KEPT, HALF), lambda n, h, info: (0, 0, part)),
         pl.BlockSpec((TOPP * RECOMP, HD), lambda n, h, info: (n, h)),
         pl.BlockSpec((TOPP * RECOMP, HD), lambda n, h, info: (n, h)),
+        pl.BlockSpec((QLEN, wide), lambda n, h, info: (n, h)),
+        pl.BlockSpec((QLEN, HD), lambda n, h, info: (n, h)),
         pl.BlockSpec((8, HD), lambda n, h, info: (0, 0)),
     ]
-    operands = [q_rows, own_kv, own_kv, kept, near, far, bound]
+    operands = [q_rows, own_kv, own_kv, kept, near, far, *own]
     aliases = {}
     if earlier is not None:
         in_specs.append(pl.BlockSpec(memory_space=pl.ANY))
@@ -306,16 +377,21 @@
     return lax.ppermute(array, axis, [(i, i ^ bits) for i in range(size)])
 
 
-def gather_columns(w_kv):
-    column = [w_kv, swap(w_kv, "member", 2), swap(w_kv, "member", 4)]
-    column.append(swap(column[2], "member", 2))
-    across = [swap(part, "group", 2) for part in column]
-    blocks, beyond = [], []
-    for k in range(4):
-        aside = swap(column[k], "member", 1)
-        blocks += [column[k], aside]
-        beyond += [across[k], swap(aside, "group", 2) if k < 3 else swap(across[k], "member", 1)]
-    return blocks, beyond
+def first_hops(w_kv):
+    return [swap(w_kv, "member", 2), swap(w_kv, "member", 4), swap(w_kv, "member", 1)]
+
+
+def gather_columns(w_kv, beyond, hops):
+    one, two, aside = hops
+    three = swap(two, "member", 2)
+    blocks, beyond = [w_kv, aside], [beyond, swap(aside, "group", 2)]
+    for part in (one, two):
+        near = swap(part, "member", 1)
+        blocks += [part, near]
+        beyond += [swap(part, "group", 2), swap(near, "group", 2)]
+    blocks += [three, swap(three, "member", 1)]
+    across = swap(three, "group", 2)
+    return blocks, beyond + [across, swap(across, "member", 1)]
 
 
 def recompute_general(normed, w_kv, pair):
@@ -345,36 +421,38 @@
     table = lax.all_to_all(request, "member", split_axis=0, concat_axis=0, tiled=True).reshape(-1)
     hidden = recomp_hidden.reshape(requests * RECOMP, D)
     normed = normalise(hidden, [])
+    me = jnp.stack([member, pair]).astype(jnp.int32)
     ahead = [normed]
+    hops = first_hops(w_kv) if tuned else []
+    ranks, passages, *hops = find_rows(table, me, holders, requests, pass_local, capacity, hops)
     if tuned:
-        blocks, beyond = gather_columns(w_kv)
-        ahead += [blocks[1], beyond[0], blocks[3], blocks[6], beyond[2]]
-    me = jnp.stack([member, pair]).astype(jnp.int32)
-    ranks, passages = find_rows(table, me, holders, requests, pass_local, capacity)
+        blocks, beyond = gather_columns(w_kv, swap(w_kv, "group", 2), hops)
+        ahead += [beyond[0], blocks[3], blocks[6], beyond[2]]
     sent = pick_rows(me, passages, ranks, cache, ahead)
     arrived = lax.all_to_all(
         sent.reshape(holders, capacity * KEPT, 2 * HALF), "member", split_axis=0, concat_axis=0, tiled=True
     ).reshape(sent.shape)
-    bound = query_bound(q_rows, [sent])
+    holder_of = wanted // pass_local
+    same = holder_of[:, None] == holder_of[None, :]
+    before = jnp.arange(requests)[None, :] < jnp.arange(requests)[:, None]
+    slot = holder_of * capacity + jnp.sum((same & before).astype(jnp.int32), axis=1)
+    flip = group // 2 if tuned else jnp.int32(0)
+    info = jnp.concatenate([jnp.stack([pair, flip]), slot]).astype(jnp.int32)
+    other_info = jnp.concatenate([jnp.stack([1 - pair, flip]), slot]).astype(jnp.int32)
+    first_own = attend_own(info, q_rows, own_kv, [sent])
     if tuned:
-        flip = group // 2
         other = swap(normed, "group", 1)
-        (begun,) = project(member, normed, other, beyond, (0, 2, 1, 4), [sent], last=False)
-        near, near_other = project(member, normed, other, blocks, tuple(range(8)), [begun])
+        (begun,) = project(member, normed, other, beyond, (0, 2, 1, 4), [first_own[0]], last=False)
+        second_own = attend_own(other_info, q_rows, own_kv, [begun])
+        near, near_other = project(member, normed, other, blocks, tuple(range(8)), [second_own[0]])
         far, far_other = project(member, normed, other, beyond, (6, 3, 5, 7), [near], carry=begun)
         first = [near, far]
         second = [swap(near_other, "group", 1), swap(far_other, "group", 1)]
     else:
-        flip = jnp.int32(0)
+        second_own = attend_own(other_info, q_rows, own_kv, [first_own[0]])
         first, second = recompute_general(normed, w_kv, pair)
-    holder_of = wanted // pass_local
-    same = holder_of[:, None] == holder_of[None, :]
-    before = jnp.arange(requests)[None, :] < jnp.arange(requests)[:, None]
-    slot = holder_of * capacity + jnp.sum((same & before).astype(jnp.int32), axis=1)
-    info = jnp.concatenate([jnp.stack([pair, flip]), slot]).astype(jnp.int32)
-    other_info = jnp.concatenate([jnp.stack([1 - pair, flip]), slot]).astype(jnp.int32)
-    out = attend(0, info, q_rows, own_kv, arrived, *first, bound)
-    return attend(1, other_info, q_rows, own_kv, arrived, *second, bound, earlier=out)
+    out = attend(0, info, q_rows, own_kv, arrived, *first, first_own)
+    return attend(1, other_info, q_rows, own_kv, arrived, *second, second_own, earlier=out)
 
 
 def solution(mesh):

time: 125 us -> 130 us (1.040)
  the two profiles are of different devices: /device:TPU:0 before, /device:TPU:31 now
where the time goes in v1:
time: 130 us; the launch traced here: 129 us
  Pallas kernels  68.3 us (53%)
  starting transfers between devices  31.5 us (24%)
  waiting for transfers between devices  20.3 us (16%)
  local copies, waits for them, and re-layouts  7.33 us (6%)
  other arithmetic  1.52 us (1%)
    pallas_call x2, Pallas kernels, attend(): pl.pallas_call(functools.partial(attend_kernel, 8), grid_spec=pltpu.Prefe...  31.8 us
    ppermute x18, waiting for transfers between devices, swap(): return lax.ppermute(array, axis, [(i, i ^ bits) for i in range(size)])  17 us
    ppermute x18, starting transfers between devices, swap(): return lax.ppermute(array, axis, [(i, i ^ bits) for i in range(size)])  16.8 us
    pallas_call x2, Pallas kernels, attend_own(): pl.pallas_call(functools.partial(own_kernel, 8), grid_spec=pltpu.Prefetch...  14.1 us
    pallas_call x3, Pallas kernels, project(): pl.pallas_call(functools.partial(project_kernel, len(weights), wanted, bo...  12.7 us
    all_to_all x1, starting transfers between devices, local(): lax.all_to_all(request, 'member', split_axis=0, concat_axis=0, tiled=True)  7.61 us
    all_to_all x1, starting transfers between devices, local(): lax.all_to_all(sent.reshape(holders, capacity * KEPT, 2 * HALF), 'member'...  7.1 us
    unnamed x46, local copies, waits for them, and re-layouts  4.57 us
  transfers between devices with their start and end apart: 20, of which 6 were waited for; matrix products, arithmetic and copies ran while one was open for 3% of the time, Pallas kernels for 38%

profile of v1, /device:TPU:31, one launch (start us, length us, event | category | flops | bytes accessed | tf_op | source)
XLA Modules:
  0.0 129.1 jit_solution(10040979808252226892)
XLA Ops:
  0.0 0.2 collective-permute-start
  0.2 0.2 collective-permute-start.2
  0.5 0.2 collective-permute-start.3
  0.7 0.8 reshape.79
  1.4 0.8 reshape.80
  2.3 0.6 broadcast_in_dim.5
  2.9 7.6 %all-to-all-start = ((s32[8,3,128]{2,1,0:T(4,128)}), s32[8,3,128]{2,1,0:T(4,128)S(1)}, u32[]{:S(2)}, u32[]{:S(2)}) async-start(s32[8,3,128]{2,1,0:T(4,128)} %broadcast_in_dim.5), calls=%async_computation | async-start | bytes 32768 | tf_op jit(solution)/shard_map/all_to_all | solution.py:421
  10.5 0.6 pad_add_fusion.1.me_ref
  11.1 3.3 %all-to-all-done = s32[8,3,128]{2,1,0:T(4,128)S(1)} async-done(((s32[8,3,128]{2,1,0:T(4,128)}), s32[8,3,128]{2,1,0:T(4,128)S(1)}, u32[]{:S(2)}, u32[]{:S(2)}) %all-to-all-start) | async-done | bytes 12320 | tf_op jit(solution)/shard_map/all_to_all | solution.py:421
  14.4 0.6 reshape.81.table_ref
  15.0 0.7 copy-done.7
  15.7 0.1 copy-done.8
  15.8 0.7 copy-done.10
  16.5 2.6 %find_rows.1 = (f32[16,64]{1,0:T(8,128)}, s32[16]{0:T(128)}, bf16[512,256]{1,0:T(8,128)(2,1)}, bf16[512,256]{1,0:T(8,128)(2,1)}, bf16[512,256]{1,0:T(8,128)(2,1)}) custom-call(s32[2]{0:T(128)} %pad_add_fusion.1.me_ref, s32[3072]{0:T(1024)} %reshape.81.table_ref, ...), custom_call_target="tpu_custom_call", output_to_operand_aliasing={{2}: (2, {}), {3}: (3, {}), {4}: (4, {})} | custom-call | flops 1 | bytes 36000000 | tf_op jit(solution)/shard_map/find_rows/pallas_call | solution.py:93
  19.1 1.1 collective-permute-start.4
  20.3 0.4 collective-permute-start.5
  20.7 4.1 %normalise.1.rest_0_.mine_ref = bf16[256,4096]{1,0:T(8,128)(2,1)} custom-call(bf16[256,4096]{1,0:T(8,128)(2,1)} %bitcast.10), custom_call_target="tpu_custom_call" | custom-call | flops 1 | bytes 1 | tf_op jit(solution)/shard_map/normalise/pallas_call | solution.py:44
  24.8 0.7 collective-permute-done.4.rest_2_.refs_3_
  25.6 0.7 collective-permute-done.5.rest_3_.refs_6_
  26.2 0.2 collective-permute-done.6.rest_4_.refs_1_
  26.4 0.5 copy-done.4
  26.9 0.2 copy-done.6
  27.1 2.8 %pick_rows.1.rest_0_ = bf16[16,48,1024]{2,1,0:T(8,128)(2,1)} custom-call(s32[2]{0:T(128)} %pad_add_fusion.1.me_ref, s32[16]{0:T(128)} %get-tuple-element.20.passage_ref, f32[16,64]{1,0:T(8,128)} %get-tuple-element.21.rank_ref, bf16[4,64,1024]{2,1,0:T(8,128)(2,1)} %cache_ref.1, bf16[256,4096]{1,0:T(8,128)(2,1)} %normalise.1.rest_0_.mine_ref, ...), custom_call_target="tpu_custom_call" | custom-call | flops 1 | bytes 1 | tf_op jit(solution)/shard_map/pick_rows/pallas_call | solution.py:126
  30.0 7.1 %all-to-all-start.1 = ((bf16[8,96,1024]{2,1,0:T(8,128)(2,1)}), bf16[8,96,1024]{2,1,0:T(8,128)(2,1)}, u32[]{:S(2)}, u32[]{:S(2)}) async-start(bf16[8,96,1024]{2,1,0:T(8,128)(2,1)} %bitcast.9), calls=%async_computation.1 | async-start | bytes 3145728 | tf_op jit(solution)/shard_map/all_to_all | solution.py:432
  37.1 3.0 %collective-permute-start.7 = (bf16[256,4096]{1,0:T(8,128)(2,1)S(1)}, bf16[256,4096]{1,0:T(8,128)(2,1)}, u32[]{:S(2)}, u32[]{:S(2)}) collective-permute-start(bf16[256,4096]{1,0:T(8,128)(2,1)S(1)} %copy-done), channel_id=1, source_target_pairs={{0,8},{8,0},{16,24},{24,16},{1,9},{9,1},{17,25},{25,17},{2,10},{10... | collective-permute-start | bytes 6291464 | tf_op jit(solution)/shard_map/ppermute | solution.py:377
  40.1 1.0 collective-permute-start.11
  41.1 0.3 collective-permute-start.8
  41.4 0.5 collective-permute-start.10
  41.9 1.0 collective-permute-start.13
  42.8 0.2 convert_reduce_fusion
  43.0 10.7 %collective-permute-done.10.refs_2_ = bf16[512,256]{1,0:T(8,128)(2,1)S(1)} collective-permute-done((bf16[512,256]{1,0:T(8,128)(2,1)S(1)}, bf16[512,256]{1,0:T(8,128)(2,1)S(1)}, u32[]{:S(2)}, u32[]{:S(2)}) %collective-permute-start.10) | collective-permute-done | bytes 262176 | tf_op jit(solution)/shard_map/ppermute | solution.py:377
  53.7 0.3 collective-permute-start.9
  54.0 1.0 collective-permute-start.14
  55.0 4.7 %collective-permute-done.8.refs_5_ = bf16[512,256]{1,0:T(8,128)(2,1)S(1)} collective-permute-done((bf16[512,256]{1,0:T(8,128)(2,1)S(1)}, bf16[512,256]{1,0:T(8,128)(2,1)S(1)}, u32[]{:S(2)}, u32[]{:S(2)}) %collective-permute-start.8) | collective-permute-done | bytes 262176 | tf_op jit(solution)/shard_map/ppermute | solution.py:377
  59.7 0.2 collective-permute-start.15
  59.9 2.2 %collective-permute-start.16 = (bf16[512,256]{1,0:T(8,128)(2,1)S(1)}, bf16[512,256]{1,0:T(8,128)(2,1)S(1)}, u32[]{:S(2)}, u32[]{:S(2)}) collective-permute-start(bf16[512,256]{1,0:T(8,128)(2,1)S(1)} %collective-permute-done.13.refs_0_), channel_id=1, source_target_pairs={{0,1},{1,0},{2,3},{3,2},{4,5},{5,4},{6,7},{7,6},{8,9},{9,8},{10,11... | collective-permute-start | bytes 786440 | tf_op jit(solution)/shard_map/ppermute | solution.py:377
  62.2 0.7 add_add_fusion.1
  62.8 7.1 %attend_own.2 = (bf16[256,4096]{1,0:T(8,128)(2,1)}, f32[256,256]{1,0:T(8,128)}, f32[8,128]{1,0:T(8,128)}) custom-call(s32[18]{0:T(128)} %get-tuple-element.35.info_ref, bf16[256,8192]{1,0:T(8,128)(2,1)} %q_ref.7, bf16[256,1024]{1,0:T(8,128)(2,1)} %own_v_ref.3, bf16[256,1024]{1,0:T(8,128)(2,1)} %own_v_ref.3, bf16[16,48,1024]{2,1,0:T(8,128)(2,1)} %pick_rows.1.rest_0_), custom_call_target="tpu_custom_call" | custom-call | flops 1 | bytes 1 | tf_op jit(solution)/shard_map/attend_own/pallas_call | solution.py:231
  69.9 4.0 %project.3.rest_0_.refs_4_ = f32[512,256]{1,0:T(8,128)} custom-call(s32[1]{0:T(128)} %bitcast.2.member_ref, bf16[256,4096]{1,0:T(8,128)(2,1)} %normalise.1.rest_0_.mine_ref, bf16[256,4096]{1,0:T(8,128)(2,1)} %collective-permute-done.7.other_ref, bf16[512,256]{1,0:T(8,128)(2,1)} %copy-done.1, bf16[512,256]{1,0:T(8,128)(2,1)} %copy-done.6, ...), custom_call_target="tpu_custom_call" | custom-call | flops 1 | bytes 18000000 | tf_op jit(solution)/shard_map/project/pallas_call | solution.py:162
  73.9 7.1 %attend_own.3 = (bf16[256,4096]{1,0:T(8,128)(2,1)}, f32[256,256]{1,0:T(8,128)}, f32[8,128]{1,0:T(8,128)}) custom-call(s32[18]{0:T(128)} %get-tuple-element.36.info_ref, bf16[256,8192]{1,0:T(8,128)(2,1)} %q_ref.7, bf16[256,1024]{1,0:T(8,128)(2,1)} %own_v_ref.3, bf16[256,1024]{1,0:T(8,128)(2,1)} %own_v_ref.3, f32[512,256]{1,0:T(8,128)} %project.3.rest_0_.refs_4_), custom_call_target="tpu_custom_call" | custom-call | flops 1 | bytes 1 | tf_op jit(solution)/shard_map/attend_own/pallas_call | solution.py:231
  81.0 0.7 copy-done.17
  81.7 4.7 %project.4 = (bf16[256,256]{1,0:T(8,128)(2,1)}, bf16[256,256]{1,0:T(8,128)(2,1)}) custom-call(s32[1]{0:T(128)} %bitcast.2.member_ref, bf16[256,4096]{1,0:T(8,128)(2,1)} %normalise.1.rest_0_.mine_ref, bf16[256,4096]{1,0:T(8,128)(2,1)} %collective-permute-done.7.other_ref, bf16[512,256]{1,0:T(8,128)(2,1)} %refs_0_.1, ...), custom_call_target="tpu_custom_call" | custom-call | flops 1 | bytes 18000000 | tf_op jit(solution)/shard_map/project/pallas_call | solution.py:162
  86.4 0.7 copy-done.14
  87.3 4.0 %project.5 = (bf16[256,256]{1,0:T(8,128)(2,1)}, bf16[256,256]{1,0:T(8,128)(2,1)}) custom-call(s32[1]{0:T(128)} %bitcast.2.member_ref, bf16[256,4096]{1,0:T(8,128)(2,1)} %normalise.1.rest_0_.mine_ref, bf16[256,4096]{1,0:T(8,128)(2,1)} %collective-permute-done.7.other_ref, bf16[512,256]{1,0:T(8,128)(2,1)} %copy-done.12, bf16[512,256]{1,0:T(8,128)(2,1)} %copy-done.14, ...), custom_call_target="tpu_custom_call" | custom-call | flops 1 | bytes 18000000 | tf_op jit(solution)/shard_map/project/pallas_call | solution.py:162
  91.3 5.1 %collective-permute-start.17 = (bf16[256,256]{1,0:T(8,128)(2,1)}, bf16[256,256]{1,0:T(8,128)(2,1)S(1)}, u32[]{:S(2)}, u32[]{:S(2)}) collective-permute-start(bf16[256,256]{1,0:T(8,128)(2,1)} %get-tuple-element.29), channel_id=1, source_target_pairs={{0,8},{8,0},{16,24},{24,16},{1,9},{9,1},{17,25},{25,17},{2,10},{10... | collective-permute-start | bytes 393224 | tf_op jit(solution)/shard_map/ppermute | solution.py:377
  96.5 15.8 %attend.2.rest_0_ = bf16[256,8192]{1,0:T(8,128)(2,1)} custom-call(s32[18]{0:T(128)} %get-tuple-element.35.info_ref, bf16[256,8192]{1,0:T(8,128)(2,1)} %q_ref.7, bf16[256,1024]{1,0:T(8,128)(2,1)} %own_v_ref.3, bf16[256,1024]{1,0:T(8,128)(2,1)} %own_v_ref.3, bf16[16,48,1024]{2,1,0:T(8,128)(2,1)} %bitcast.7.kept_ref, ...), custom_call_target="tpu_custom_call" | custom-call | flops 1 | bytes 1 | tf_op jit(solution)/shard_map/attend/pallas_call | solution.py:354
  112.4 0.6 copy-done.20
  113.0 16.0 %attend.3 = bf16[256,8192]{1,0:T(8,128)(2,1)} custom-call(s32[18]{0:T(128)} %get-tuple-element.36.info_ref, bf16[256,8192]{1,0:T(8,128)(2,1)} %q_ref.7, bf16[256,1024]{1,0:T(8,128)(2,1)} %own_v_ref.3, bf16[256,1024]{1,0:T(8,128)(2,1)} %own_v_ref.3, bf16[16,48,1024]{2,1,0:T(8,128)(2,1)} %bitcast.7.kept_ref, ...), custom_call_target="tpu_custom_call", output_to_operand_aliasing={{}: (10, {})} | custom-call | flops 1 | bytes 1 | tf_op jit(solution)/shard_map/attend/pallas_call | solution.py:354
  (59 shorter events, 0.7 us)
Async XLA Ops:
  0.0 15.0 %collective-permute-start = (bf16[512,256]{1,0:T(8,128)(2,1)}, bf16[512,256]{1,0:T(8,128)(2,1)S(1)}, u32[]{:S(2)}, u32[]{:S(2)}) collective-permute-start(bf16[512,256]{1,0:T(8,128)(2,1)} %refs_0_.1), channel_id=1, source_target_pairs={{0,2},{1,3},{2,0},{3,1},{4,6},{5,7},{6,4},{7,5},{8,10},{9,11},{10,... | collective-permute-start | bytes 786440 | tf_op jit(solution)/shard_map/ppermute | solution.py:377
  0.2 14.8 %collective-permute-start.1 = (bf16[512,256]{1,0:T(8,128)(2,1)}, bf16[512,256]{1,0:T(8,128)(2,1)S(1)}, u32[]{:S(2)}, u32[]{:S(2)}) collective-permute-start(bf16[512,256]{1,0:T(8,128)(2,1)} %refs_0_.1), channel_id=1, source_target_pairs={{0,4},{1,5},{2,6},{3,7},{4,0},{5,1},{6,2},{7,3},{8,12},{9,13},{10,... | collective-permute-start | bytes 786440 | tf_op jit(solution)/shard_map/ppermute | solution.py:377
  0.2 14.8 %collective-permute-start.2 = (bf16[512,256]{1,0:T(8,128)(2,1)}, bf16[512,256]{1,0:T(8,128)(2,1)S(1)}, u32[]{:S(2)}, u32[]{:S(2)}) collective-permute-start(bf16[512,256]{1,0:T(8,128)(2,1)} %refs_0_.1), channel_id=1, source_target_pairs={{0,1},{1,0},{2,3},{3,2},{4,5},{5,4},{6,7},{7,6},{8,9},{9,8},{10,11... | collective-permute-start | bytes 786440 | tf_op jit(solution)/shard_map/ppermute | solution.py:377
  0.5 24.4 %collective-permute-start.3 = (bf16[512,256]{1,0:T(8,128)(2,1)}, bf16[512,256]{1,0:T(8,128)(2,1)S(1)}, u32[]{:S(2)}, u32[]{:S(2)}) collective-permute-start(bf16[512,256]{1,0:T(8,128)(2,1)} %refs_0_.1), channel_id=1, source_target_pairs={{0,16},{8,24},{16,0},{24,8},{1,17},{9,25},{17,1},{25,9},{2,18},{10... | collective-permute-start | bytes 786440 | tf_op jit(solution)/shard_map/ppermute | solution.py:377
  2.9 11.5 %all-to-all-start = ((s32[8,3,128]{2,1,0:T(4,128)}), s32[8,3,128]{2,1,0:T(4,128)S(1)}, u32[]{:S(2)}, u32[]{:S(2)}) async-start(s32[8,3,128]{2,1,0:T(4,128)} %broadcast_in_dim.5), calls=%async_computation | async-start | bytes 32768 | tf_op jit(solution)/shard_map/all_to_all | solution.py:421
  15.0 0.7 copy-start.7
  15.0 0.8 copy-start.8
  15.8 0.7 copy-start.10
  19.1 6.4 %collective-permute-start.4 = (bf16[512,256]{1,0:T(8,128)(2,1)}, bf16[512,256]{1,0:T(8,128)(2,1)S(1)}, u32[]{:S(2)}, u32[]{:S(2)}) collective-permute-start(bf16[512,256]{1,0:T(8,128)(2,1)} %get-tuple-element.22.refs_2_), channel_id=1, source_target_pairs={{0,1},{1,0},{2,3},{3,2},{4,5},{5,4},{6,7},{7,6},{8,9},{9,8},{10,11... | collective-permute-start | bytes 786440 | tf_op jit(solution)/shard_map/ppermute | solution.py:377
  20.3 6.0 %collective-permute-start.5 = (bf16[512,256]{1,0:T(8,128)(2,1)}, bf16[512,256]{1,0:T(8,128)(2,1)S(1)}, u32[]{:S(2)}, u32[]{:S(2)}) collective-permute-start(bf16[512,256]{1,0:T(8,128)(2,1)} %get-tuple-element.23.refs_4_), channel_id=1, source_target_pairs={{0,2},{1,3},{2,0},{3,1},{4,6},{5,7},{6,4},{7,5},{8,10},{9,11},{10,... | collective-permute-start | bytes 786440 | tf_op jit(solution)/shard_map/ppermute | solution.py:377
  20.6 5.8 %collective-permute-start.6 = (bf16[512,256]{1,0:T(8,128)(2,1)}, bf16[512,256]{1,0:T(8,128)(2,1)S(1)}, u32[]{:S(2)}, u32[]{:S(2)}) collective-permute-start(bf16[512,256]{1,0:T(8,128)(2,1)} %get-tuple-element.22.refs_2_), channel_id=1, source_target_pairs={{0,16},{8,24},{16,0},{24,8},{1,17},{9,25},{17,1},{25,9},{2,18},{10... | collective-permute-start | bytes 786440 | tf_op jit(solution)/shard_map/ppermute | solution.py:377
  24.8 1.6 %copy-start.1 = (bf16[512,256]{1,0:T(8,128)(2,1)}, bf16[512,256]{1,0:T(8,128)(2,1)S(1)}, u32[]{:S(2)}) copy-start(bf16[512,256]{1,0:T(8,128)(2,1)S(1)} %collective-permute-done.3.rest_1_.refs_0_) | copy-start | bytes 786436
  25.6 0.8 copy-start.2
  26.2 0.7 copy-start.4
  26.4 0.7 copy-start.6
  30.0 7.1 %copy-start = (bf16[256,4096]{1,0:T(8,128)(2,1)S(1)}, bf16[256,4096]{1,0:T(8,128)(2,1)}, u32[]{:S(2)}) copy-start(bf16[256,4096]{1,0:T(8,128)(2,1)} %normalise.1.rest_0_.mine_ref) | copy-start | bytes 6291460
  30.0 10.1 %copy-start.9 = (bf16[512,256]{1,0:T(8,128)(2,1)S(1)}, bf16[512,256]{1,0:T(8,128)(2,1)}, u32[]{:S(2)}) copy-start(bf16[512,256]{1,0:T(8,128)(2,1)} %get-tuple-element.23.refs_4_) | copy-start | bytes 786436
  30.0 11.4 %copy-start.11 = (bf16[512,256]{1,0:T(8,128)(2,1)S(1)}, bf16[512,256]{1,0:T(8,128)(2,1)}, u32[]{:S(2)}) copy-start(bf16[512,256]{1,0:T(8,128)(2,1)} %get-tuple-element.24.refs_1_) | copy-start | bytes 786436
  30.0 11.9 %copy-start.5 = (bf16[512,256]{1,0:T(8,128)(2,1)S(1)}, bf16[512,256]{1,0:T(8,128)(2,1)}, u32[]{:S(2)}) copy-start(bf16[512,256]{1,0:T(8,128)(2,1)} %copy-done.4) | copy-start | bytes 786436
  30.0 24.0 %copy-start.3 = (bf16[512,256]{1,0:T(8,128)(2,1)S(1)}, bf16[512,256]{1,0:T(8,128)(2,1)}, u32[]{:S(2)}) copy-start(bf16[512,256]{1,0:T(8,128)(2,1)} %copy-done.2) | copy-start | bytes 786436
  30.0 66.5 %all-to-all-start.1 = ((bf16[8,96,1024]{2,1,0:T(8,128)(2,1)}), bf16[8,96,1024]{2,1,0:T(8,128)(2,1)}, u32[]{:S(2)}, u32[]{:S(2)}) async-start(bf16[8,96,1024]{2,1,0:T(8,128)(2,1)} %bitcast.9), calls=%async_computation.1 | async-start | bytes 3145728 | tf_op jit(solution)/shard_map/all_to_all | solution.py:432
  37.1 32.8 %collective-permute-start.7 = (bf16[256,4096]{1,0:T(8,128)(2,1)S(1)}, bf16[256,4096]{1,0:T(8,128)(2,1)}, u32[]{:S(2)}, u32[]{:S(2)}) collective-permute-start(bf16[256,4096]{1,0:T(8,128)(2,1)S(1)} %copy-done), channel_id=1, source_target_pairs={{0,8},{8,0},{16,24},{24,16},{1,9},{9,1},{17,25},{25,17},{2,10},{10... | collective-permute-start | bytes 6291464 | tf_op jit(solution)/shard_map/ppermute | solution.py:377
  40.1 13.9 %collective-permute-start.11 = (bf16[512,256]{1,0:T(8,128)(2,1)S(1)}, bf16[512,256]{1,0:T(8,128)(2,1)S(1)}, u32[]{:S(2)}, u32[]{:S(2)}) collective-permute-start(bf16[512,256]{1,0:T(8,128)(2,1)S(1)} %copy-done.9), channel_id=1, source_target_pairs={{0,16},{8,24},{16,0},{24,8},{1,17},{9,25},{17,1},{25,9},{2,18},{10... | collective-permute-start | bytes 786440 | tf_op jit(solution)/shard_map/ppermute | solution.py:377
  41.1 18.7 %collective-permute-start.8 = (bf16[512,256]{1,0:T(8,128)(2,1)S(1)}, bf16[512,256]{1,0:T(8,128)(2,1)S(1)}, u32[]{:S(2)}, u32[]{:S(2)}) collective-permute-start(bf16[512,256]{1,0:T(8,128)(2,1)S(1)} %copy-done.9), channel_id=1, source_target_pairs={{0,1},{1,0},{2,3},{3,2},{4,5},{5,4},{6,7},{7,6},{8,9},{9,8},{10,11... | collective-permute-start | bytes 786440 | tf_op jit(solution)/shard_map/ppermute | solution.py:377
  41.4 12.3 %collective-permute-start.10 = (bf16[512,256]{1,0:T(8,128)(2,1)S(1)}, bf16[512,256]{1,0:T(8,128)(2,1)S(1)}, u32[]{:S(2)}, u32[]{:S(2)}) collective-permute-start(bf16[512,256]{1,0:T(8,128)(2,1)S(1)} %copy-done.11), channel_id=1, source_target_pairs={{0,16},{8,24},{16,0},{24,8},{1,17},{9,25},{17,1},{25,9},{2,18},{10... | collective-permute-start | bytes 786440 | tf_op jit(solution)/shard_map/ppermute | solution.py:377
  41.9 18.1 %collective-permute-start.13 = (bf16[512,256]{1,0:T(8,128)(2,1)S(1)}, bf16[512,256]{1,0:T(8,128)(2,1)S(1)}, u32[]{:S(2)}, u32[]{:S(2)}) collective-permute-start(bf16[512,256]{1,0:T(8,128)(2,1)S(1)} %copy-done.5), channel_id=1, source_target_pairs={{0,16},{8,24},{16,0},{24,8},{1,17},{9,25},{17,1},{25,9},{2,18},{10... | collective-permute-start | bytes 786440 | tf_op jit(solution)/shard_map/ppermute | solution.py:377
  53.7 16.2 %copy-start.19 = (bf16[512,256]{1,0:T(8,128)(2,1)}, bf16[512,256]{1,0:T(8,128)(2,1)S(1)}, u32[]{:S(2)}) copy-start(bf16[512,256]{1,0:T(8,128)(2,1)S(1)} %collective-permute-done.10.refs_2_) | copy-start | bytes 786436
  53.7 27.3 %collective-permute-start.9 = (bf16[512,256]{1,0:T(8,128)(2,1)S(1)}, bf16[512,256]{1,0:T(8,128)(2,1)S(1)}, u32[]{:S(2)}, u32[]{:S(2)}) collective-permute-start(bf16[512,256]{1,0:T(8,128)(2,1)S(1)} %copy-done.5), channel_id=1, source_target_pairs={{0,1},{1,0},{2,3},{3,2},{4,5},{5,4},{6,7},{7,6},{8,9},{9,8},{10,11... | collective-permute-start | bytes 786440 | tf_op jit(solution)/shard_map/ppermute | solution.py:377
  54.0 15.9 %copy-start.15 = (bf16[512,256]{1,0:T(8,128)(2,1)}, bf16[512,256]{1,0:T(8,128)(2,1)S(1)}, u32[]{:S(2)}) copy-start(bf16[512,256]{1,0:T(8,128)(2,1)S(1)} %collective-permute-done.11.refs_3_) | copy-start | bytes 786436
  54.0 32.4 %collective-permute-start.14 = (bf16[512,256]{1,0:T(8,128)(2,1)S(1)}, bf16[512,256]{1,0:T(8,128)(2,1)S(1)}, u32[]{:S(2)}, u32[]{:S(2)}) collective-permute-start(bf16[512,256]{1,0:T(8,128)(2,1)S(1)} %copy-done.3), channel_id=1, source_target_pairs={{0,16},{8,24},{16,0},{24,8},{1,17},{9,25},{17,1},{25,9},{2,18},{10... | collective-permute-start | bytes 786440 | tf_op jit(solution)/shard_map/ppermute | solution.py:377
  59.7 10.1 %copy-start.13 = (bf16[512,256]{1,0:T(8,128)(2,1)}, bf16[512,256]{1,0:T(8,128)(2,1)S(1)}, u32[]{:S(2)}) copy-start(bf16[512,256]{1,0:T(8,128)(2,1)S(1)} %collective-permute-done.8.refs_5_) | copy-start | bytes 786436
  59.7 26.7 %collective-permute-start.15 = (bf16[512,256]{1,0:T(8,128)(2,1)S(1)}, bf16[512,256]{1,0:T(8,128)(2,1)S(1)}, u32[]{:S(2)}, u32[]{:S(2)}) collective-permute-start(bf16[512,256]{1,0:T(8,128)(2,1)S(1)} %collective-permute-done.8.refs_5_), channel_id=1, source_target_pairs={{0,16},{8,24},{16,0},{24,8},{1,17},{9,25},{17,1},{25,9},{2,18},{10... | collective-permute-start | bytes 786440 | tf_op jit(solution)/shard_map/ppermute | solution.py:377
  59.9 9.9 %copy-start.12 = (bf16[512,256]{1,0:T(8,128)(2,1)}, bf16[512,256]{1,0:T(8,128)(2,1)S(1)}, u32[]{:S(2)}) copy-start(bf16[512,256]{1,0:T(8,128)(2,1)S(1)} %collective-permute-done.13.refs_0_) | copy-start | bytes 786436
  59.9 26.5 %collective-permute-start.16 = (bf16[512,256]{1,0:T(8,128)(2,1)S(1)}, bf16[512,256]{1,0:T(8,128)(2,1)S(1)}, u32[]{:S(2)}, u32[]{:S(2)}) collective-permute-start(bf16[512,256]{1,0:T(8,128)(2,1)S(1)} %collective-permute-done.13.refs_0_), channel_id=1, source_target_pairs={{0,1},{1,0},{2,3},{3,2},{4,5},{5,4},{6,7},{7,6},{8,9},{9,8},{10,11... | collective-permute-start | bytes 786440 | tf_op jit(solution)/shard_map/ppermute | solution.py:377
  81.0 0.7 copy-start.17
  86.4 0.7 copy-start.14
  86.4 0.8 copy-start.16
  86.4 0.9 copy-start.18
  87.3 9.1 %copy-start.22 = (bf16[256,256]{1,0:T(8,128)(2,1)S(1)}, bf16[256,256]{1,0:T(8,128)(2,1)}, u32[]{:S(2)}) copy-start(bf16[256,256]{1,0:T(8,128)(2,1)} %get-tuple-element.27) | copy-start | bytes 393220
  91.3 21.0 %collective-permute-start.17 = (bf16[256,256]{1,0:T(8,128)(2,1)}, bf16[256,256]{1,0:T(8,128)(2,1)S(1)}, u32[]{:S(2)}, u32[]{:S(2)}) collective-permute-start(bf16[256,256]{1,0:T(8,128)(2,1)} %get-tuple-element.29), channel_id=1, source_target_pairs={{0,8},{8,0},{16,24},{24,16},{1,9},{9,1},{17,25},{25,17},{2,10},{10... | collective-permute-start | bytes 393224 | tf_op jit(solution)/shard_map/ppermute | solution.py:377
  96.4 15.9 %collective-permute-start.12 = (bf16[256,256]{1,0:T(8,128)(2,1)S(1)}, bf16[256,256]{1,0:T(8,128)(2,1)S(1)}, u32[]{:S(2)}, u32[]{:S(2)}) collective-permute-start(bf16[256,256]{1,0:T(8,128)(2,1)S(1)} %copy-done.22), channel_id=1, source_target_pairs={{0,8},{8,0},{16,24},{24,16},{1,9},{9,1},{17,25},{25,17},{2,10},{10... | collective-permute-start | bytes 393224 | tf_op jit(solution)/shard_map/ppermute | solution.py:377
  112.3 0.7 copy-start.20
  112.3 0.7 copy-start.21
